TPU v7x, 256 devices: a whole 4x4x8 slice. The times are simulated.
256 devices in a mesh: boxes: 128 (over z, x, y), dirs: 2 (over core).
Axes of the slice: x: 4, y: 4, z: 8, core: 2. Of those that a mesh axis runs over, the one named last changes fastest.
Arguments:
- points: bfloat16 [4096, 2, 192], P('boxes', 'dirs'), may hold values from -1 to 1
- charges: bfloat16 [4096, 2, 4, 128], P('boxes', 'dirs'), may hold values from -6 to 6
- near_box: int32 [4096, 27], P('boxes'), may hold values from 0 to 4095, as said below
- near_code: int32 [4096, 27], P('boxes'), may hold values from 0 to 26
- send_box: int32 [16384, 16], P('boxes'), may hold values from 0 to 31
- far_slot: int32 [4096, 128], P('boxes'), may hold values from 0 to 2047, as said below
- far_direction: int32 [4096, 128], P('boxes'), may hold values from 0 to 15
- coarse_source: int32 [512, 32], P('boxes'), may hold values from 0 to 511
- coarse_direction: int32 [512, 32], P('boxes'), may hold values from 0 to 15
- leaf_translate: bfloat16 [16, 256, 256], P('dirs'), may hold values from -0.5 to 0.5
- coarse_translate: bfloat16 [16, 256, 256], P('dirs'), may hold values from -0.375 to 0.375
- child_to_parent: bfloat16 [8, 256, 256], replicated, may hold values from -0.375 to 0.375
- parent_to_child: bfloat16 [8, 256, 256], replicated, may hold values from -0.1875 to 0.1875
Outputs:
- potential: bfloat16 [4096, 2, 4, 128], P('boxes', 'dirs')
Inputs may be any that keep to these rules, and one draw needn't show every extreme that they name: `near_box`: every entry names a box at most 8 places from the box itself along the curve; each box has entries 8 places before and after it wherever such boxes exist. `far_slot`: A value s * 16 + c names slot c of the buffer that device s sends to the device holding the box; where c >= 7, s is at most 2 devices from that device. Every slot allowed so is named by some entry of that device's boxes.
All inputs are finite; a program needn't handle non-finite values.
Results may differ from a plain program's by a relative error of at most 0.009.
Values may be sent and summed in bfloat16 or wider, within the bound.
A program may use at most 64 MiB of HBM per device.

v0:
```python
import jax
import jax.numpy as jnp
from jax import lax
from jax.sharding import PartitionSpec as P

PTS = 128
EQ = 128
DIRS = 16
RHS = 4
NEAR = 27
CAP = 16
HB = 8
PAR_DEV = 4


wave_number = 3.0
smoothing = 0.0625
sphere_radius = 2.5
golden_turn = 2.399963229728653
four_pi = 12.566370614359172


def with_halo(cells, sides, width):
    for axis, dim in sides:
        count = lax.axis_size(axis)
        ends = count - 1
        head = lax.slice_in_dim(cells, 0, width, axis=dim)
        tail = lax.slice_in_dim(cells, cells.shape[dim] - width, cells.shape[dim], axis=dim)
        cells = jnp.concatenate(
            [
                lax.ppermute(tail, axis, [(i, (i + 1) % count) for i in range(ends)]),
                cells,
                lax.ppermute(head, axis, [((i + 1) % count, i) for i in range(ends)]),
            ],
            axis=dim,
        )
    return cells


def surface_points():
    ordinal = jnp.arange(EQ).astype(jnp.float32)
    height = 1.0 - (2.0 * ordinal + 1.0) / EQ
    radial = jnp.sqrt(1.0 - height * height)
    angles = ordinal * golden_turn
    return sphere_radius * jnp.stack([radial * jnp.cos(angles), radial * jnp.sin(angles), height])


def kernel_parts(squared):
    spread = jnp.sqrt(squared + smoothing)
    amplitude = 1.0 / (four_pi * spread)
    return (
        (amplitude * jnp.cos(wave_number * spread)).astype(jnp.bfloat16),
        (amplitude * jnp.sin(wave_number * spread)).astype(jnp.bfloat16),
    )


def code_offsets(code_block):
    return 2.0 * jnp.stack(
        [code_block // 9 - 1, code_block // 3 % 3 - 1, code_block % 3 - 1], axis=-1
    ).astype(jnp.float32)


def contract_up(kern, charge):
    return jnp.einsum("nep,nrp->nre", kern, charge, preferred_element_type=jnp.float32)


def contract_down(kern, value):
    return jnp.einsum("nep,nre->nrp", kern, value, preferred_element_type=jnp.float32)


def near_contract(kern, charge):
    return jnp.einsum("gkps,gkrs->grp", kern, charge, preferred_element_type=jnp.float32)


def on_device(
    points,
    charges,
    near_box,
    near_code,
    send_box,
    far_slot,
    far_direction,
    coarse_source,
    coarse_direction,
    leaf_translate,
    coarse_translate,
    child_to_parent,
    parent_to_child,
):
    boxes_here = points.shape[0]
    halves = lax.axis_size("dirs")
    half_pts = points.shape[2] // 3
    rhs_half = RHS // halves
    device = lax.axis_index("boxes")
    peer_count = lax.axis_size("boxes")
    surface = surface_points()
    my_pos = points[:, 0, :].astype(jnp.float32).reshape(boxes_here, 3, half_pts)
    differences = surface[None, :, :, None] - my_pos[:, :, None, :]
    kern_real, kern_imag = kernel_parts(jnp.sum(differences * differences, axis=1))
    mine_real = charges[:, 0, :, :half_pts]
    mine_imag = charges[:, 0, :, half_pts:]
    part_real = contract_up(kern_real, mine_real) - contract_up(kern_imag, mine_imag)
    part_imag = contract_up(kern_real, mine_imag) + contract_up(kern_imag, mine_real)
    partial_value = jnp.concatenate([part_real, part_imag], axis=-1)
    outgoing = lax.psum_scatter(partial_value, "dirs", scatter_dimension=1, tiled=True).astype(
        jnp.bfloat16
    )
    grouped = outgoing.reshape(PAR_DEV, 8, rhs_half, 2 * EQ)
    parent = jnp.einsum(
        "cork,okj->crj", grouped, child_to_parent, preferred_element_type=jnp.float32
    ).astype(jnp.bfloat16)
    outbound = outgoing[send_box]
    arrived = lax.all_to_all(outbound, "boxes", split_axis=0, concat_axis=0, tiled=True)
    gathered = arrived.reshape(peer_count * CAP, rhs_half * 2 * EQ)[far_slot]
    all_directions = jnp.arange(DIRS, dtype=jnp.int32)
    direction_hot = (far_direction[:, :, None] == all_directions[None, None, :]).astype(
        jnp.bfloat16
    )
    leaf_cone = (
        jnp.einsum("bld,blk->dbk", direction_hot, gathered, preferred_element_type=jnp.float32)
        .astype(jnp.bfloat16)
        .reshape(DIRS, boxes_here, rhs_half, 2 * EQ)
    )
    parent_hot = (coarse_direction[:, :, None] == all_directions[None, None, :]).astype(
        jnp.bfloat16
    )
    shard_rows = lax.all_gather(parent, "boxes", axis=0, tiled=True)
    number = shard_rows.shape[0]
    wanted = (
        coarse_source[:, :, None] == jnp.arange(number, dtype=jnp.int32)[None, None, :]
    ).astype(jnp.bfloat16)
    weights = jnp.einsum(
        "cld,clj->dcj", parent_hot, wanted, preferred_element_type=jnp.float32
    ).astype(jnp.bfloat16)
    coarse_total = jnp.einsum(
        "dcj,jk->dck",
        weights,
        shard_rows.reshape(number, rhs_half * 2 * EQ),
        preferred_element_type=jnp.float32,
    )
    coarse_cone = coarse_total.astype(jnp.bfloat16).reshape(DIRS, PAR_DEV, rhs_half, 2 * EQ)
    leaf_table, coarse_table = (
        lax.all_gather(leaf_translate, "dirs", axis=0, tiled=True),
        lax.all_gather(coarse_translate, "dirs", axis=0, tiled=True),
    )
    coarse_local = jnp.einsum(
        "dcrk,dkj->crj", coarse_cone, coarse_table, preferred_element_type=jnp.float32
    ).astype(jnp.bfloat16)
    leaf_part = jnp.einsum(
        "dbrk,dkj->brj", leaf_cone, leaf_table, preferred_element_type=jnp.float32
    )
    child_terms = jnp.einsum(
        "crk,okj->corj", coarse_local, parent_to_child, preferred_element_type=jnp.float32
    ).reshape(boxes_here, rhs_half, 2 * EQ)
    local_half = (leaf_part + child_terms).astype(jnp.bfloat16)
    local_exp = lax.all_gather(local_half, "dirs", axis=1, tiled=True)
    local_real = local_exp[:, :, :EQ]
    local_imag = local_exp[:, :, EQ:]
    far_real = contract_down(kern_real, local_real) - contract_down(kern_imag, local_imag)
    far_imag = contract_down(kern_imag, local_real) + contract_down(kern_real, local_imag)
    all_points, all_charges = (
        lax.all_gather(points, "dirs", axis=1, tiled=True),
        lax.all_gather(charges, "dirs", axis=1, tiled=True),
    )
    sources = jnp.concatenate(
        [all_points, all_charges.reshape(boxes_here, halves, RHS * 2 * half_pts)], axis=-1
    )
    padded = with_halo(sources, (("boxes", 0),), HB)
    row_ids = near_box - (device * boxes_here - HB)
    picked = padded[row_ids]
    source_pos = jnp.transpose(
        picked[..., : 3 * half_pts]
        .astype(jnp.float32)
        .reshape(boxes_here, NEAR, halves, 3, half_pts),
        (0, 1, 3, 2, 4),
    ).reshape(boxes_here, NEAR, 3, PTS)
    source_charge = picked[..., 3 * half_pts :].reshape(boxes_here, NEAR, halves, RHS, 2, half_pts)
    source_real = jnp.transpose(source_charge[:, :, :, :, 0, :], (0, 1, 3, 2, 4)).reshape(
        boxes_here, NEAR, RHS, PTS
    )
    source_imag = jnp.transpose(source_charge[:, :, :, :, 1, :], (0, 1, 3, 2, 4)).reshape(
        boxes_here, NEAR, RHS, PTS
    )

    def near_group(inputs):
        targets, group_pos, code_block, group_real, group_imag = inputs
        shifted = group_pos + code_offsets(code_block)[..., None]
        gaps = targets[:, None, :, :, None] - shifted[:, :, :, None, :]
        kern_near_real, kern_near_imag = kernel_parts(jnp.sum(gaps * gaps, axis=2))
        near_real = near_contract(kern_near_real, group_real) - near_contract(
            kern_near_imag, group_imag
        )
        near_imag = near_contract(kern_near_imag, group_real) + near_contract(
            kern_near_real, group_imag
        )
        return (near_real, near_imag)

    groups = boxes_here // 8
    near_real, near_imag = lax.map(
        near_group,
        (
            my_pos.reshape(groups, 8, 3, half_pts),
            source_pos.reshape(groups, 8, NEAR, 3, PTS),
            near_code.reshape(groups, 8, NEAR),
            source_real.reshape(groups, 8, NEAR, RHS, PTS),
            source_imag.reshape(groups, 8, NEAR, RHS, PTS),
        ),
    )
    total_real = far_real + near_real.reshape(boxes_here, RHS, half_pts)
    total_imag = far_imag + near_imag.reshape(boxes_here, RHS, half_pts)
    return jnp.concatenate([total_real, total_imag], axis=-1).astype(jnp.bfloat16)[:, None]


def solution(mesh):
    return jax.shard_map(
        on_device,
        mesh=mesh,
        in_specs=(
            P("boxes", "dirs", None),
            P("boxes", "dirs", None, None),
            P("boxes", None),
            P("boxes", None),
            P("boxes", None),
            P("boxes", None),
            P("boxes", None),
            P("boxes", None),
            P("boxes", None),
            P("dirs", None, None),
            P("dirs", None, None),
            P(),
            P(),
        ),
        out_specs=P("boxes", "dirs", None, None),
        check_vma=False,
    )
```

profile of v0, /device:TPU:1, one launch (start us, length us, event | category | flops | bytes accessed | tf_op | source)
XLA Modules:
  0.0 672.3 jit_solution(8154400808903549980)
XLA Ops:
  8.6 4.3 multiply_convert_fusion.3
  16.5 4.7 all_gather.23
  24.6 4.5 collective-permute-start
  29.8 8.8 %gather_fusion.2 = bf16[864,2,704]{2,1,0:T(2,128)(2,1)} fusion(bf16[48,2,704]{2,1,0:T(2,128)(2,1)S(1)} %pad_maximum_fusion, s32[1024]{0:T(1024)S(1)} %pad_clamp_fusion), kind=kCustom, calls=%fused_computation.2 | custom fusion | bytes 4869504 | tf_op jit(solution)/shard_map/gather | solution.py:170
  38.6 5.1 slice.50
  43.7 2.7 slice.52
  46.8 3.3 reshape.358
  50.0 8.6 %fusion.80 = (bf16[32,27,2,4,1,64]{5,4,3,0,2,1:T(2,128)(2,1)S(1)}, bf16[32,27,2,4,1,64]{5,4,3,0,2,1:T(2,128)(2,1)S(1)}) fusion(bf16[32,27,2,4,2,64]{5,4,3,0,2,1:T(2,128)(2,1)} %reshape.358), kind=kLoop, calls=%fused_computation.127 | loop fusion | bytes 3538944 | tf_op jit(solution)/shard_map/slice | solution.py:181
  58.6 2.3 copy_bitcast_fusion
  60.9 3.1 copy.183
  64.0 3.9 reshape.410
  69.4 4.7 reshape.366
  74.1 5.7 copy.184
  79.7 4.9 reshape.411
  84.6 4.5 copy.185
  89.2 3.7 reshape.412
  93.8 16.4 %gather_fusion = bf16[2048,2,256]{2,1,0:T(2,128)(2,1)} fusion(bf16[32,2,256]{2,1,0:T(2,128)(2,1)S(1)} %copy.210, s32[2048]{0:T(1024)S(1)} %broadcast_clamp_fusion), kind=kCustom, calls=%fused_computation | custom fusion | bytes 4202496 | tf_op jit(solution)/shard_map/gather | solution.py:112
  110.2 19.7 %all-to-all-start = ((bf16[128,16,2,256]{3,2,1,0:T(2,128)(2,1)}), bf16[128,16,2,256]{3,2,1,0:T(2,128)(2,1)}, u32[]{:S(2)}, u32[]{:S(2)}) async-start(bf16[128,16,2,256]{3,2,1,0:T(2,128)(2,1)} %bitcast.252), calls=%async_computation.1 | async-start | bytes 4194304 | tf_op jit(solution)/shard_map/all_to_all | solution.py:113
  129.9 152.3 %while.15 = (s32[]{:T(128)}, f32[4,8,4,64]{3,2,1,0:T(4,128)S(1)}, f32[4,8,4,64]{3,2,1,0:T(4,128)S(1)}, bf16[4,8,27,4,128]{4,3,2,1,0:T(4,128)(2,1)S(1)}, f32[4,8,...) while((s32[]{:T(128)}, f32[4,8,4,64]{3,2,1,0:T(4,128)S(1)}, ...), condition=%wide.region_4.5_spmd, body=%wide.region_2.4_spmd.sunk | while | flops 85030120 | bytes 37389740 | solution.py:199
  131.5 3.9 multiply_reduce_fusion.3
  135.4 28.3 %multiply_convert_fusion.5 = (bf16[8,27,64,128]{3,2,1,0:T(8,128)(2,1)S(1)}, bf16[8,27,64,128]{3,2,1,0:T(8,128)(2,1)S(1)}) fusion(f32[8,27,64,128]{3,2,1,0:T(8,128)S(1)} %multiply_reduce_fusion.3), kind=kLoop, calls=%fused_computation.4.clone.1 | loop fusion | flops 14155776 | bytes 14155776 | tf_op jit(solution)/shard_map/while/body/eval_jaxpr/convert_element_type | solution.py:53
  169.6 3.9 multiply_reduce_fusion.3
  173.5 28.3 %multiply_convert_fusion.5 = (bf16[8,27,64,128]{3,2,1,0:T(8,128)(2,1)S(1)}, bf16[8,27,64,128]{3,2,1,0:T(8,128)(2,1)S(1)}) fusion(f32[8,27,64,128]{3,2,1,0:T(8,128)S(1)} %multiply_reduce_fusion.3), kind=kLoop, calls=%fused_computation.4.clone.1 | loop fusion | flops 14155776 | bytes 14155776 | tf_op jit(solution)/shard_map/while/body/eval_jaxpr/convert_element_type | solution.py:53
  207.6 3.9 multiply_reduce_fusion.3
  211.6 28.3 %multiply_convert_fusion.5 = (bf16[8,27,64,128]{3,2,1,0:T(8,128)(2,1)S(1)}, bf16[8,27,64,128]{3,2,1,0:T(8,128)(2,1)S(1)}) fusion(f32[8,27,64,128]{3,2,1,0:T(8,128)S(1)} %multiply_reduce_fusion.3), kind=kLoop, calls=%fused_computation.4.clone.1 | loop fusion | flops 14155776 | bytes 14155776 | tf_op jit(solution)/shard_map/while/body/eval_jaxpr/convert_element_type | solution.py:53
  245.7 3.9 multiply_reduce_fusion.3
  249.7 28.3 %multiply_convert_fusion.5 = (bf16[8,27,64,128]{3,2,1,0:T(8,128)(2,1)S(1)}, bf16[8,27,64,128]{3,2,1,0:T(8,128)(2,1)S(1)}) fusion(f32[8,27,64,128]{3,2,1,0:T(8,128)S(1)} %multiply_reduce_fusion.3), kind=kLoop, calls=%fused_computation.4.clone.1 | loop fusion | flops 14155776 | bytes 14155776 | tf_op jit(solution)/shard_map/while/body/eval_jaxpr/convert_element_type | solution.py:53
  283.8 292.3 %all_gather.19 = bf16[512,2,256]{2,1,0:T(2,128)(2,1)S(1)} all-gather(bf16[4,2,256]{2,1,0:T(2,128)(2,1)S(1)} %fusion.53), channel_id=1, replica_groups=mesh['boxes'=128,'dirs'=2] {'boxes'}, dimensions={0}, use_global_device_ids=true | all-gather | bytes 528384 | tf_op jit(solution)/shard_map/all_gather | solution.py:127
  581.7 17.3 %gather_fusion.1 = bf16[4096,512]{1,0:T(8,128)(2,1)} fusion(bf16[2048,512]{1,0:T(8,128)(2,1)S(1)} %bitcast.246, s32[4096]{0:T(1024)S(1)} %fusion.75), kind=kCustom, calls=%fused_computation.1 | custom fusion | bytes 8404992 | tf_op jit(solution)/shard_map/gather | solution.py:114
  599.0 2.9 fusion.31
  602.1 2.2 fusion.43
  604.3 59.0 %all_gather.21 = bf16[32,4,256]{2,0,1:T(8,128)(2,1)S(1)} all-gather(bf16[32,2,256]{2,0,1:T(8,128)(2,1)S(1)} %fusion.43), channel_id=1, replica_groups=mesh['boxes'=128,'dirs'=2] {'dirs'}, dimensions={1}, use_global_device_ids=true | all-gather | bytes 98304 | tf_op jit(solution)/shard_map/all_gather | solution.py:156
  (127 shorter events, 45.1 us)
Async XLA Ops:
  6.5 572.9 %copy-start = (bf16[8,256,256]{2,1,0:T(8,128)(2,1)S(1)}, bf16[8,256,256]{2,1,0:T(8,128)(2,1)}, u32[]{:S(2)}) copy-start(bf16[8,256,256]{2,1,0:T(8,128)(2,1)} %param.27) | copy-start | bytes 3145732
  6.5 7.6 %copy-start.6 = (bf16[32,1,4,128]{3,2,1,0:T(4,128)(2,1)S(1)}, bf16[32,1,4,128]{3,2,1,0:T(4,128)(2,1)}, u32[]{:S(2)}) copy-start(bf16[32,1,4,128]{3,2,1,0:T(4,128)(2,1)} %param.16) | copy-start | bytes 98308
  6.5 86.3 %reduce-scatter.2.cloned.1.call-start = ((), (), s32[]{:S(2)}) async-start(), calls=%async_computation.2 | async-start | bytes 196608 | tf_op jit(solution)/shard_map/reduce_scatter | solution.py:105
  8.6 12.7 %copy-start.7 = (bf16[32,1,192]{2,0,1:T(8,128)(2,1)S(1)}, bf16[32,1,192]{2,0,1:T(8,128)(2,1)}, u32[]{:S(2)}) copy-start(bf16[32,1,192]{2,0,1:T(8,128)(2,1)} %param.15) | copy-start | bytes 36868
  8.6 20.5 %copy-start.10 = (s32[32,27]{1,0:T(8,128)S(1)}, s32[32,27]{1,0:T(8,128)}, u32[]{:S(2)}) copy-start(s32[32,27]{1,0:T(8,128)} %param.17) | copy-start | bytes 10372
  8.6 20.6 %copy-start.12 = (s32[128,16]{0,1:T(8,128)S(1)}, s32[128,16]{0,1:T(8,128)}, u32[]{:S(2)}) copy-start(s32[128,16]{0,1:T(8,128)} %param.19) | copy-start | bytes 24580
  12.9 1.7 copy-start.1
  12.9 2.0 copy-start.3
  13.0 16.5 %copy-start.11 = (s32[32,128]{1,0:T(8,128)S(1)}, s32[32,128]{1,0:T(8,128)}, u32[]{:S(2)}) copy-start(s32[32,128]{1,0:T(8,128)} %param.20) | copy-start | bytes 49156
  15.7 561.6 %all-gather.5.cloned.1.call-start = ((), (), s32[]{:S(2)}) async-start(), calls=%async_computation.4 | async-start | bytes 3145728 | tf_op jit(solution)/shard_map/all_gather | solution.py:144
  16.5 585.6 %all-gather.3.cloned.1.call-start = ((), (), s32[]{:S(2)}) async-start(), calls=%async_computation.3 | async-start | bytes 3145728 | tf_op jit(solution)/shard_map/all_gather | solution.py:143
  23.3 6.3 collective-permute-start.1
  24.6 5.0 collective-permute-start
  60.9 7.0 %copy-start.5 = (bf16[32,27,2,192]{3,2,1,0:T(2,128)(2,1)S(1)}, bf16[32,27,2,192]{3,2,1,0:T(2,128)(2,1)}, u32[]{:S(2)}) copy-start(bf16[32,27,2,192]{3,2,1,0:T(2,128)(2,1)} %slice.52) | copy-start | bytes 1990660
  93.8 36.1 %copy-start.8 = (s32[32,27]{1,0:T(8,128)S(1)}, s32[32,27]{1,0:T(8,128)}, u32[]{:S(2)}) copy-start(s32[32,27]{1,0:T(8,128)} %param.18) | copy-start | bytes 10372
  110.2 469.5 %all-to-all-start = ((bf16[128,16,2,256]{3,2,1,0:T(2,128)(2,1)}), bf16[128,16,2,256]{3,2,1,0:T(2,128)(2,1)}, u32[]{:S(2)}, u32[]{:S(2)}) async-start(bf16[128,16,2,256]{3,2,1,0:T(2,128)(2,1)} %bitcast.252), calls=%async_computation.1 | async-start | bytes 4194304 | tf_op jit(solution)/shard_map/all_to_all | solution.py:113
  282.2 294.6 %copy-start.13 = (s32[4,32]{1,0:T(4,128)S(1)}, s32[4,32]{1,0:T(4,128)}, u32[]{:S(2)}) copy-start(s32[4,32]{1,0:T(4,128)} %param.22) | copy-start | bytes 1540
  282.2 294.6 %copy-start.14 = (s32[4,32]{1,0:T(4,128)S(1)}, s32[4,32]{1,0:T(4,128)}, u32[]{:S(2)}) copy-start(s32[4,32]{1,0:T(4,128)} %param.23) | copy-start | bytes 1540
  581.7 17.3 %copy-start.9 = (s32[32,128]{1,0:T(8,128)S(1)}, s32[32,128]{1,0:T(8,128)}, u32[]{:S(2)}) copy-start(s32[32,128]{1,0:T(8,128)} %param.21) | copy-start | bytes 49156
  599.0 64.3 %copy-start.2 = (bf16[32,128,64]{1,2,0:T(8,128)(2,1)S(1)}, bf16[32,128,64]{1,2,0:T(8,128)(2,1)}, u32[]{:S(2)}) copy-start(bf16[32,128,64]{1,2,0:T(8,128)(2,1)} %copy-done.1) | copy-start | bytes 1572868
  599.0 64.7 %copy-start.4 = (bf16[32,128,64]{1,2,0:T(8,128)(2,1)S(1)}, bf16[32,128,64]{1,2,0:T(8,128)(2,1)}, u32[]{:S(2)}) copy-start(bf16[32,128,64]{1,2,0:T(8,128)(2,1)} %copy-done.3) | copy-start | bytes 1572868
Sparse Core Ops, SparseCore 0:
  15.8 17.3 reduce-scatter.1
  35.0 17.1 all-gather.4
  54.1 17.1 all-gather.2
where the time goes:
time: 676 us; the launch traced here: 672 us
  blocking collectives  358 us (53%)
  other arithmetic  142 us (21%)
  local copies, waits for them, and re-layouts  102 us (15%)
  matrix products  30.1 us (4%)
  starting transfers between devices  25.5 us (4%)
  between operations  13.8 us (2%)
    all_gather x1, blocking collectives, on_device(): shard_rows = lax.all_gather(parent, 'boxes', axis=0, tiled=True)  292 us
    convert_element_type x4, other arithmetic, kernel_parts(): (amplitude * jnp.sin(wave_number * spread)).astype(jnp.bfloat16)  113 us
    all_gather x1, blocking collectives, on_device(): local_exp = lax.all_gather(local_half, 'dirs', axis=1, tiled=True)  59 us
    while x6, local copies, waits for them, and re-layouts, on_device(): lax.map(near_group, (my_pos.reshape(groups, 8, 3, half_pts), source_pos.r...  25.7 us
    all_to_all x1, starting transfers between devices, on_device(): lax.all_to_all(outbound, 'boxes', split_axis=0, concat_axis=0, tiled=True)  19.7 us
    gather x1, local copies, waits for them, and re-layouts, on_device(): gathered = arrived.reshape(peer_count * CAP, rhs_half * 2 * EQ)[far_slot]  17.3 us
    dot_general x16, matrix products, near_contract(): jnp.einsum('gkps,gkrs->grp', kern, charge, preferred_element_type=jnp.flo...  17.2 us
    gather x1, local copies, waits for them, and re-layouts, on_device(): outbound = outgoing[send_box]  16.4 us
  transfers between devices with their start and end apart: 6, of which 0 were waited for; matrix products, arithmetic and copies ran while one was open for 39% of the time, Pallas kernels for 0%

commit v1 on v0

--- a/solution.py
+++ b/solution.py
@@ -1,6 +1,12 @@
+import functools
+import math
+
 import jax
 import jax.numpy as jnp
+import numpy as np
 from jax import lax
+from jax.experimental import pallas as pl
+from jax.experimental.pallas import tpu as pltpu
 from jax.sharding import PartitionSpec as P
 
 PTS = 128
@@ -54,12 +60,6 @@
     )
 
 
-def code_offsets(code_block):
-    return 2.0 * jnp.stack(
-        [code_block // 9 - 1, code_block // 3 % 3 - 1, code_block % 3 - 1], axis=-1
-    ).astype(jnp.float32)
-
-
 def contract_up(kern, charge):
     return jnp.einsum("nep,nrp->nre", kern, charge, preferred_element_type=jnp.float32)
 
@@ -68,8 +68,136 @@
     return jnp.einsum("nep,nre->nrp", kern, value, preferred_element_type=jnp.float32)
 
 
-def near_contract(kern, charge):
-    return jnp.einsum("gkps,gkrs->grp", kern, charge, preferred_element_type=jnp.float32)
+FEATURES = 16
+TURNS = 3.0 / (2.0 * math.pi)
+COS_TERMS = (0.99999922, -19.73898252, 64.92872662, -85.27239703, 58.79403881, -21.07678228)
+SIN_TERMS = (6.2830558, -41.33121431, 81.36681533, -74.47800473, 32.78140114)
+AMPLITUDE = TURNS / four_pi
+
+
+def split3(values):
+    high = values.astype(jnp.bfloat16).astype(jnp.float32)
+    rest = values - high
+    middle = rest.astype(jnp.bfloat16).astype(jnp.float32)
+    return high, middle, rest - middle
+
+
+def horner(terms, z):
+    total = z * (AMPLITUDE * terms[-1]) + AMPLITUDE * terms[-2]
+    for term in terms[-3::-1]:
+        total = total * z + AMPLITUDE * term
+    return total
+
+
+def wave(scaled):
+    inverse = lax.rsqrt(scaled)
+    phase = scaled * inverse
+    phase = phase - jnp.round(phase)
+    z = phase * phase
+    return inverse * horner(COS_TERMS, z), (inverse * phase) * horner(SIN_TERMS, z)
+
+
+def coordinates(first, second):
+    return [
+        jnp.concatenate([first[:, k * 64 : k * 64 + 64], second[:, k * 64 : k * 64 + 64]], axis=1)
+        for k in range(3)
+    ]
+
+
+def source_features(coords):
+    square = TURNS * TURNS * sum(c * c for c in coords)
+    one = jnp.ones_like(square)
+    return coords * 3 + list(split3(square)) + [one, one, one, jnp.zeros_like(one)]
+
+
+def target_features(coords):
+    scale = TURNS * TURNS
+    square = scale * (sum(c * c for c in coords) + smoothing)
+    one = jnp.ones_like(square)
+    parts = [split3(-2.0 * scale * c) for c in coords]
+    rows = [parts[k][i] for i in range(3) for k in range(3)]
+    return rows + [one, one, one] + list(split3(square)) + [jnp.zeros_like(one)]
+
+
+def near_kernel(box_ref, code_ref, pos_ref, charge_ref, out_ref, rows_ref, source_ref, target_ref, dense_ref):
+    half_boxes = out_ref.shape[0]
+    boxes = pos_ref.shape[1]
+    coords = coordinates(pos_ref[0].astype(jnp.float32), pos_ref[1].astype(jnp.float32))
+    for f, row in enumerate(source_features(coords)):
+        rows_ref[pl.ds(f, boxes, stride=FEATURES), :] = row
+
+    def turn(j, carry):
+        tile = rows_ref[pl.ds(pl.multiple_of(j * FEATURES, FEATURES), FEATURES), :]
+        source_ref[pl.ds(pl.multiple_of(j * PTS, PTS), PTS), :] = tile.T.astype(jnp.bfloat16)
+        return carry
+
+    lax.fori_loop(0, boxes, turn, 0)
+    mine = [c[HB : HB + half_boxes] for c in coords]
+    for code in range(27):
+        offset = (2.0 * (code // 9 - 1), 2.0 * (code // 3 % 3 - 1), 2.0 * (code % 3 - 1))
+        moved = [c - o for c, o in zip(mine, offset)]
+        for f, row in enumerate(target_features(moved)):
+            target_ref[pl.ds(code * half_boxes * FEATURES + f, half_boxes, stride=FEATURES), :] = row
+
+    lane = lax.broadcasted_iota(jnp.int32, (4, 128), 1)
+    sign = jnp.where(lane < 64, 1.0, -1.0)
+
+    def weigh(j, carry):
+        parts = []
+        for h in range(2):
+            q = charge_ref[h, j].astype(jnp.float32)
+            parts.append(jnp.concatenate([q * sign, pltpu.roll(q, 64, 1)], axis=0))
+        both = jnp.concatenate(parts, axis=1)
+        dense_ref[pl.ds(pl.multiple_of(j * 16, 16), 16), :] = jnp.concatenate(
+            [both, jnp.zeros_like(both)], axis=0
+        ).astype(jnp.bfloat16)
+        return carry
+
+    lax.fori_loop(0, boxes, weigh, 0)
+
+    def one_box(b, carry):
+        def group(g, total):
+            for i in range(9):
+                n = g * 9 + i
+                j = box_ref[b, n]
+                code = code_ref[b, n]
+                y = source_ref[pl.ds(pl.multiple_of(j * PTS, PTS), PTS), :]
+                x = target_ref[
+                    pl.ds(pl.multiple_of((code * half_boxes + b) * FEATURES, FEATURES), FEATURES), :
+                ].astype(jnp.bfloat16)
+                real, imag = wave(jnp.dot(y, x, preferred_element_type=jnp.float32))
+                real, imag = real.astype(jnp.bfloat16), imag.astype(jnp.bfloat16)
+                kern = jnp.concatenate([real[:64], imag[:64], real[64:], imag[64:]], axis=0)
+                q = dense_ref[pl.ds(pl.multiple_of(j * 16, 16), 16), :]
+                total = total + jnp.dot(q, kern, preferred_element_type=jnp.float32)
+            return total
+
+        total = lax.fori_loop(0, 3, group, jnp.zeros((16, PTS), jnp.float32))
+        out_ref[b] = total[:8]
+        return carry
+
+    lax.fori_loop(0, half_boxes, one_box, 0)
+
+
+def near_call(boxes_in, codes, positions, charges):
+    half_boxes, boxes = boxes_in.shape[0], positions.shape[1]
+    vmem = pl.BlockSpec(memory_space=pltpu.VMEM)
+    smem = pl.BlockSpec(memory_space=pltpu.SMEM)
+    return pl.pallas_call(
+        near_kernel,
+        out_shape=jax.ShapeDtypeStruct((half_boxes, 8, PTS), jnp.float32),
+        in_specs=[smem, smem, vmem, vmem],
+        out_specs=vmem,
+        scratch_shapes=[
+            pltpu.VMEM((boxes * FEATURES, 128), jnp.float32),
+            pltpu.VMEM((boxes * PTS, FEATURES), jnp.bfloat16),
+            pltpu.VMEM((27 * half_boxes * FEATURES, 128), jnp.float32),
+            pltpu.VMEM((boxes * 16, 256), jnp.bfloat16),
+        ],
+        compiler_params=pltpu.CompilerParams(vmem_limit_bytes=40 * 1024 * 1024),
+        cost_estimate=pl.CostEstimate(flops=10**9, bytes_accessed=10**6, transcendentals=0),
+        name="near_field",
+    )(boxes_in, codes, positions, charges)
 
 
 def on_device(
@@ -109,8 +237,15 @@
     parent = jnp.einsum(
         "cork,okj->crj", grouped, child_to_parent, preferred_element_type=jnp.float32
     ).astype(jnp.bfloat16)
-    outbound = outgoing[send_box]
-    arrived = lax.all_to_all(outbound, "boxes", split_axis=0, concat_axis=0, tiled=True)
+    outbound = jnp.concatenate(
+        [
+            outgoing[send_box],
+            jnp.broadcast_to(parent[None], (peer_count,) + parent.shape),
+        ],
+        axis=1,
+    )
+    received = lax.all_to_all(outbound, "boxes", split_axis=0, concat_axis=0, tiled=True)
+    arrived = received[:, :CAP]
     gathered = arrived.reshape(peer_count * CAP, rhs_half * 2 * EQ)[far_slot]
     all_directions = jnp.arange(DIRS, dtype=jnp.int32)
     direction_hot = (far_direction[:, :, None] == all_directions[None, None, :]).astype(
@@ -124,7 +259,7 @@
     parent_hot = (coarse_direction[:, :, None] == all_directions[None, None, :]).astype(
         jnp.bfloat16
     )
-    shard_rows = lax.all_gather(parent, "boxes", axis=0, tiled=True)
+    shard_rows = received[:, CAP:].reshape(peer_count * PAR_DEV, rhs_half, 2 * EQ)
     number = shard_rows.shape[0]
     wanted = (
         coarse_source[:, :, None] == jnp.arange(number, dtype=jnp.int32)[None, None, :]
@@ -166,48 +301,24 @@
         [all_points, all_charges.reshape(boxes_here, halves, RHS * 2 * half_pts)], axis=-1
     )
     padded = with_halo(sources, (("boxes", 0),), HB)
-    row_ids = near_box - (device * boxes_here - HB)
-    picked = padded[row_ids]
-    source_pos = jnp.transpose(
-        picked[..., : 3 * half_pts]
-        .astype(jnp.float32)
-        .reshape(boxes_here, NEAR, halves, 3, half_pts),
-        (0, 1, 3, 2, 4),
-    ).reshape(boxes_here, NEAR, 3, PTS)
-    source_charge = picked[..., 3 * half_pts :].reshape(boxes_here, NEAR, halves, RHS, 2, half_pts)
-    source_real = jnp.transpose(source_charge[:, :, :, :, 0, :], (0, 1, 3, 2, 4)).reshape(
-        boxes_here, NEAR, RHS, PTS
-    )
-    source_imag = jnp.transpose(source_charge[:, :, :, :, 1, :], (0, 1, 3, 2, 4)).reshape(
-        boxes_here, NEAR, RHS, PTS
-    )
-
-    def near_group(inputs):
-        targets, group_pos, code_block, group_real, group_imag = inputs
-        shifted = group_pos + code_offsets(code_block)[..., None]
-        gaps = targets[:, None, :, :, None] - shifted[:, :, :, None, :]
-        kern_near_real, kern_near_imag = kernel_parts(jnp.sum(gaps * gaps, axis=2))
-        near_real = near_contract(kern_near_real, group_real) - near_contract(
-            kern_near_imag, group_imag
-        )
-        near_imag = near_contract(kern_near_imag, group_real) + near_contract(
-            kern_near_real, group_imag
-        )
-        return (near_real, near_imag)
-
-    groups = boxes_here // 8
-    near_real, near_imag = lax.map(
-        near_group,
-        (
-            my_pos.reshape(groups, 8, 3, half_pts),
-            source_pos.reshape(groups, 8, NEAR, 3, PTS),
-            near_code.reshape(groups, 8, NEAR),
-            source_real.reshape(groups, 8, NEAR, RHS, PTS),
-            source_imag.reshape(groups, 8, NEAR, RHS, PTS),
-        ),
-    )
-    total_real = far_real + near_real.reshape(boxes_here, RHS, half_pts)
-    total_imag = far_imag + near_imag.reshape(boxes_here, RHS, half_pts)
+    core = lax.axis_index("dirs")
+    half_boxes = boxes_here // halves
+    window = lax.dynamic_slice_in_dim(padded, core * half_boxes, half_boxes + 2 * HB, 0)
+    window = jnp.transpose(window, (1, 0, 2))
+    rows = lax.dynamic_slice_in_dim(near_box, core * half_boxes, half_boxes, 0)
+    rows = rows - (device * boxes_here + core * half_boxes - HB)
+    codes = lax.dynamic_slice_in_dim(near_code, core * half_boxes, half_boxes, 0)
+    near = near_call(
+        rows,
+        codes,
+        window[:, :, : 3 * half_pts],
+        window[:, :, 3 * half_pts :].reshape(halves, half_boxes + 2 * HB, RHS, 2 * half_pts),
+    )
+    near = lax.all_gather(near, "dirs", axis=0, tiled=True)
+    near = lax.dynamic_slice_in_dim(near, core * half_pts, half_pts, 2)
+    near_real, near_imag = near[:, :RHS], near[:, RHS:]
+    total_real = far_real + near_real
+    total_imag = far_imag + near_imag
     return jnp.concatenate([total_real, total_imag], axis=-1).astype(jnp.bfloat16)[:, None]
 
 

time: 676 us -> 211 us (0.31)
  the two profiles are of different devices: /device:TPU:1 before, /device:TPU:97 now
where the time goes in v1:
time: 211 us; the launch traced here: 210 us
  waiting for transfers between devices  62 us (29%)
  Pallas kernels  44.9 us (21%)
  local copies, waits for them, and re-layouts  34.9 us (17%)
  starting transfers between devices  23.3 us (11%)
  between operations  13.5 us (6%)
  matrix products  11.9 us (6%)
  other arithmetic  11.3 us (5%)
  blocking collectives  8.69 us (4%)
    ppermute x1, waiting for transfers between devices, with_halo(): lax.ppermute(tail, axis, [(i, (i + 1) % count) for i in range(ends)])  45.5 us
    pallas_call x1, Pallas kernels, near_call(): pl.pallas_call(near_kernel, out_shape=jax.ShapeDtypeStruct((half_boxes, 8...  44.9 us
    gather x1, local copies, waits for them, and re-layouts, on_device(): gathered = arrived.reshape(peer_count * CAP, rhs_half * 2 * EQ)[far_slot]  17.4 us
    reduce_scatter x1, waiting for transfers between devices, on_device(): lax.psum_scatter(partial_value, 'dirs', scatter_dimension=1, tiled=True)  15.1 us
    all_to_all x1, starting transfers between devices, on_device(): lax.all_to_all(outbound, 'boxes', split_axis=0, concat_axis=0, tiled=True)  13.7 us
    gather x1, local copies, waits for them, and re-layouts, on_device(): outgoing[send_box]  7.91 us
    ppermute x1, starting transfers between devices, with_halo(): lax.ppermute(head, axis, [((i + 1) % count, i) for i in range(ends)])  6.4 us
    concatenate x1, other arithmetic, on_device(): jnp.concatenate([outgoing[send_box], jnp.broadcast_to(parent[None], (peer...  4.87 us
  transfers between devices with their start and end apart: 6, of which 2 were waited for; matrix products, arithmetic and copies ran while one was open for 14% of the time, Pallas kernels for 21%

profile of v1, /device:TPU:97, one launch (start us, length us, event | category | flops | bytes accessed | tf_op | source)
XLA Modules:
  0.0 210.5 jit_solution(8262016572243602082)
XLA Ops:
  6.6 0.9 reshape.134
  7.5 1.0 multiply_reduce_fusion
  8.6 4.3 %multiply_convert_fusion.1 = (bf16[32,128,64]{1,2,0:T(8,128)(2,1)S(1)}, bf16[32,128,64]{1,2,0:T(8,128)(2,1)S(1)}) fusion(f32[32,128,64]{1,2,0:T(8,128)S(1)} %multiply_reduce_fusion), kind=kLoop, calls=%fused_computation.37 | loop fusion | flops 2097152 | bytes 2097152 | tf_op jit(solution)/shard_map/convert_element_type | solution.py:58
  13.2 0.5 copy-done.1
  14.6 0.7 copy.68
  15.5 15.1 %reduce-scatter.2.cloned.1.call-done = f32[32,2,256]{2,0,1:T(8,128)} async-done(((f32[32,4,256]{2,0,1:T(8,128)}), f32[32,2,256]{2,0,1:T(8,128)}) %reduce-scatter.2.cloned.1.call-update) | async-done | bytes 65552 | tf_op jit(solution)/shard_map/reduce_scatter | solution.py:233
  30.7 0.9 copy.102
  31.6 7.9 %gather_fusion = bf16[2048,2,256]{2,1,0:T(2,128)(2,1)S(1)} fusion(bf16[32,2,256]{2,1,0:T(2,128)(2,1)S(1)} %copy.102, s32[2048]{0:T(1024)S(1)} %broadcast_clamp_fusion), kind=kCustom, calls=%fused_computation | custom fusion | bytes 4202496 | tf_op jit(solution)/shard_map/gather | solution.py:242
  39.5 1.5 fusion.26
  41.3 4.9 %pad_maximum_fusion = bf16[128,20,2,256]{3,2,1,0:T(2,128)(2,1)} fusion(bf16[128,4,2,256]{3,2,1,0:T(2,128)(2,1)S(1)} %broadcast_in_dim.7, bf16[128,16,2,256]{3,2,1,0:T(2,128)(2,1)S(1)} %bitcast.108), kind=kLoop, calls=%fused_computation.3 | loop fusion | flops 1310720 | bytes 5242880 | tf_op jit(solution)/shard_map/concatenate | solution.py:240
  46.1 13.7 %all-to-all-start = ((bf16[128,20,2,256]{3,2,1,0:T(2,128)(2,1)}), bf16[128,20,2,256]{3,2,1,0:T(2,128)(2,1)}, u32[]{:S(2)}, u32[]{:S(2)}) async-start(bf16[128,20,2,256]{3,2,1,0:T(2,128)(2,1)} %pad_maximum_fusion), calls=%async_computation.1 | async-start | bytes 5242880 | tf_op jit(solution)/shard_map/all_to_all | solution.py:247
  59.9 0.7 all-gather.5.cloned.1.call-update
  60.7 0.7 all-gather.3.cloned.1.call-update
  61.4 2.3 %all_gather.22 = bf16[32,2,4,128]{3,2,1,0:T(4,128)(2,1)S(1)} all-gather(bf16[32,1,4,128]{3,2,1,0:T(4,128)(2,1)S(1)} %copy-done.5), channel_id=1, replica_groups=mesh['boxes'=128,'dirs'=2] {'dirs'}, dimensions={1}, use_global_device_ids=true | all-gather | bytes 98304 | tf_op jit(solution)/shard_map/all_gather | solution.py:298
  63.7 1.8 all_gather.21
  65.6 3.1 %collective-permute-start = (bf16[8,2,704]{2,0,1:T(8,128)(2,1)S(1)}, bf16[8,2,704]{2,0,1:T(8,128)(2,1)S(1)}, u32[]{:S(2)}, u32[]{:S(2)}) collective-permute-start(bf16[8,2,704]{2,0,1:T(8,128)(2,1)S(1)} %get-tuple-element.8), channel_id=1, source_target_pairs={{0,2},{2,4},{4,6},{6,8},{8,10},{10,12},{12,14},{14,16},{16,18},{18... | collective-permute-start | bytes 67592 | tf_op jit(solution)/shard_map/ppermute | solution.py:37
  68.7 6.4 %collective-permute-start.1 = (bf16[8,2,704]{2,0,1:T(8,128)(2,1)S(1)}, bf16[8,2,704]{2,0,1:T(8,128)(2,1)S(1)}, u32[]{:S(2)}, u32[]{:S(2)}) collective-permute-start(bf16[8,2,704]{2,0,1:T(8,128)(2,1)S(1)} %get-tuple-element.7), channel_id=1, source_target_pairs={{2,0},{4,2},{6,4},{8,6},{10,8},{12,10},{14,12},{16,14},{18,16},{20... | collective-permute-start | bytes 67592 | tf_op jit(solution)/shard_map/ppermute | solution.py:39
  75.2 45.5 %collective-permute-done = bf16[8,2,704]{2,0,1:T(8,128)(2,1)S(1)} collective-permute-done((bf16[8,2,704]{2,0,1:T(8,128)(2,1)S(1)}, bf16[8,2,704]{2,0,1:T(8,128)(2,1)S(1)}, u32[]{:S(2)}, u32[]{:S(2)}) %collective-permute-start) | collective-permute-done | bytes 22560 | tf_op jit(solution)/shard_map/ppermute | solution.py:37
  120.9 44.9 %near_field.1 = f32[16,8,128]{2,1,0:T(8,128)S(1)} custom-call(s32[16,27]{1,0:T(8,128)S(1)} %get-tuple-element.13.box_ref, s32[16,27]{1,0:T(8,128)S(1)} %get-tuple-element.14.code_ref, bf16[2,32,192]{2,1,0:T(8,128)(2,1)S(1)} %slice.58.pos_ref, bf16[2,32,4,128]{3,2,1,0:T(4,128)(2,1)S(1)} %reshape.133.charge_ref), custom_call_target="tpu_custom_call" | custom-call | flops 1000000000 | bytes 1000000 | tf_op jit(solution)/shard_map/near_field/pallas_call | solution.py:186
  165.8 2.7 %all_gather.23 = f32[32,8,128]{2,1,0:T(8,128)S(1)} all-gather(f32[16,8,128]{2,1,0:T(8,128)S(1)} %near_field.1), channel_id=1, replica_groups=mesh['boxes'=128,'dirs'=2] {'dirs'}, dimensions={0}, use_global_device_ids=true | all-gather | bytes 196608 | tf_op jit(solution)/shard_map/all_gather | solution.py:317
  168.6 3.6 %slice.54 = bf16[128,16,2,256]{3,2,1,0:T(2,128)(2,1)S(1)} slice(bf16[128,20,2,256]{3,2,1,0:T(2,128)(2,1)} %all-to-all-done), slice={[0:128], [0:16], [0:2], [0:256]} | slice | bytes 4194304 | tf_op jit(solution)/shard_map/slice | solution.py:248
  172.1 0.5 copy.87
  172.7 17.4 %gather_fusion.1 = bf16[4096,512]{1,0:T(8,128)(2,1)} fusion(bf16[2048,512]{1,0:T(8,128)(2,1)S(1)} %bitcast.105, s32[4096]{0:T(1024)S(1)} %fusion.52), kind=kCustom, calls=%fused_computation.1 | custom fusion | bytes 8404992 | tf_op jit(solution)/shard_map/gather | solution.py:249
  190.0 2.8 %fusion.4 = bf16[16,32,512]{2,0,1:T(8,128)(2,1)S(1)} fusion(bf16[32,128,512]{2,1,0:T(8,128)(2,1)} %bitcast.107, s32[32,128]{1,0:T(8,128)S(1)} %copy-done.7), kind=kOutput, calls=%fused_computation.9 | convolution fusion | flops 67436544 | bytes 4734976 | tf_op jit(solution)/shard_map/bld,blk->dbk/dot_general | solution.py:255
  193.0 1.4 slice.55
  195.2 2.0 fusion.30
  197.6 2.2 %fusion.16 = bf16[32,2,256]{2,0,1:T(8,128)(2,1)S(1)} fusion(bf16[16,256,256]{2,1,0:T(8,128)(2,1)} %all-gather.3.cloned.1.call-done, bf16[16,32,2,256]{3,2,0,1:T(2,128)(2,1)S(1)} %reshape.129, f32[4,8,2,256]{3,0,1,2:T(4,128)S(1)} %convolution_bitcast_fusion), kind=kOutput, calls=%fused_computation.24 | convolution fusion | flops 134250496 | bytes 2719744 | tf_op jit(solution)/shard_map/dbrk,dkj->brj/dot_general | solution.py:284
  199.8 1.9 all_gather.20
  202.1 0.4 fusion.47
  202.4 0.4 fusion.21
  202.8 0.4 fusion.22
  203.2 0.7 maximum_bitcast_fusion
  (64 shorter events, 3.7 us)
Async XLA Ops:
  6.5 190.7 %copy-start = (bf16[8,256,256]{2,1,0:T(8,128)(2,1)S(1)}, bf16[8,256,256]{2,1,0:T(8,128)(2,1)}, u32[]{:S(2)}) copy-start(bf16[8,256,256]{2,1,0:T(8,128)(2,1)} %param.25) | copy-start | bytes 3145732
  6.5 6.4 %copy-start.5 = (bf16[32,1,4,128]{3,2,1,0:T(4,128)(2,1)S(1)}, bf16[32,1,4,128]{3,2,1,0:T(4,128)(2,1)}, u32[]{:S(2)}) copy-start(bf16[32,1,4,128]{3,2,1,0:T(4,128)(2,1)} %param.14) | copy-start | bytes 98308
  6.5 24.1 %reduce-scatter.2.cloned.1.call-start = ((), (), s32[]{:S(2)}) async-start(), calls=%async_computation.2 | async-start | bytes 196608 | tf_op jit(solution)/shard_map/reduce_scatter | solution.py:233
  8.6 6.8 %copy-start.9 = (s32[128,16]{0,1:T(8,128)S(1)}, s32[128,16]{0,1:T(8,128)}, u32[]{:S(2)}) copy-start(s32[128,16]{0,1:T(8,128)} %param.17) | copy-start | bytes 24580
  12.9 0.8 copy-start.1
  12.9 1.4 copy-start.3
  46.1 17.5 %copy-start.6 = (bf16[32,1,192]{2,0,1:T(8,128)(2,1)S(1)}, bf16[32,1,192]{2,0,1:T(8,128)(2,1)}, u32[]{:S(2)}) copy-start(bf16[32,1,192]{2,0,1:T(8,128)(2,1)} %param.13) | copy-start | bytes 36868
  46.1 122.4 %all-to-all-start = ((bf16[128,20,2,256]{3,2,1,0:T(2,128)(2,1)}), bf16[128,20,2,256]{3,2,1,0:T(2,128)(2,1)}, u32[]{:S(2)}, u32[]{:S(2)}) async-start(bf16[128,20,2,256]{3,2,1,0:T(2,128)(2,1)} %pad_maximum_fusion), calls=%async_computation.1 | async-start | bytes 5242880 | tf_op jit(solution)/shard_map/all_to_all | solution.py:247
  59.8 15.3 %copy-start.8 = (s32[32,128]{1,0:T(8,128)S(1)}, s32[32,128]{1,0:T(8,128)}, u32[]{:S(2)}) copy-start(s32[32,128]{1,0:T(8,128)} %param.18) | copy-start | bytes 49156
  59.8 15.3 %copy-start.10 = (s32[32,27]{1,0:T(8,128)S(1)}, s32[32,27]{1,0:T(8,128)}, u32[]{:S(2)}) copy-start(s32[32,27]{1,0:T(8,128)} %param.15) | copy-start | bytes 10372
  59.9 15.3 %copy-start.11 = (s32[32,27]{1,0:T(8,128)S(1)}, s32[32,27]{1,0:T(8,128)}, u32[]{:S(2)}) copy-start(s32[32,27]{1,0:T(8,128)} %param.16) | copy-start | bytes 10372
  59.9 135.4 %all-gather.5.cloned.1.call-start = ((), (), s32[]{:S(2)}) async-start(), calls=%async_computation.4 | async-start | bytes 3145728 | tf_op jit(solution)/shard_map/all_gather | solution.py:279
  60.6 136.9 %all-gather.3.cloned.1.call-start = ((), (), s32[]{:S(2)}) async-start(), calls=%async_computation.3 | async-start | bytes 3145728 | tf_op jit(solution)/shard_map/all_gather | solution.py:278
  65.6 55.1 %collective-permute-start = (bf16[8,2,704]{2,0,1:T(8,128)(2,1)S(1)}, bf16[8,2,704]{2,0,1:T(8,128)(2,1)S(1)}, u32[]{:S(2)}, u32[]{:S(2)}) collective-permute-start(bf16[8,2,704]{2,0,1:T(8,128)(2,1)S(1)} %get-tuple-element.8), channel_id=1, source_target_pairs={{0,2},{2,4},{4,6},{6,8},{8,10},{10,12},{12,14},{14,16},{16,18},{18... | collective-permute-start | bytes 67592 | tf_op jit(solution)/shard_map/ppermute | solution.py:37
  68.7 52.0 %collective-permute-start.1 = (bf16[8,2,704]{2,0,1:T(8,128)(2,1)S(1)}, bf16[8,2,704]{2,0,1:T(8,128)(2,1)S(1)}, u32[]{:S(2)}, u32[]{:S(2)}) collective-permute-start(bf16[8,2,704]{2,0,1:T(8,128)(2,1)S(1)} %get-tuple-element.7), channel_id=1, source_target_pairs={{2,0},{4,2},{6,4},{8,6},{10,8},{12,10},{14,12},{16,14},{18,16},{20... | collective-permute-start | bytes 67592 | tf_op jit(solution)/shard_map/ppermute | solution.py:39
  172.7 17.4 %copy-start.7 = (s32[32,128]{1,0:T(8,128)S(1)}, s32[32,128]{1,0:T(8,128)}, u32[]{:S(2)}) copy-start(s32[32,128]{1,0:T(8,128)} %param.19) | copy-start | bytes 49156
  192.9 1.9 copy-start.12
  192.9 1.9 copy-start.13
  197.3 4.4 %copy-start.2 = (bf16[32,128,64]{1,2,0:T(8,128)(2,1)S(1)}, bf16[32,128,64]{1,2,0:T(8,128)(2,1)}, u32[]{:S(2)}) copy-start(bf16[32,128,64]{1,2,0:T(8,128)(2,1)} %copy-done.1) | copy-start | bytes 1572868
  197.3 4.8 %copy-start.4 = (bf16[32,128,64]{1,2,0:T(8,128)(2,1)S(1)}, bf16[32,128,64]{1,2,0:T(8,128)(2,1)}, u32[]{:S(2)}) copy-start(bf16[32,128,64]{1,2,0:T(8,128)(2,1)} %copy-done.3) | copy-start | bytes 1572868
Sparse Core Ops, SparseCore 0:
  15.5 15.1 reduce-scatter.1
  62.5 17.7 all-gather.4
  82.1 17.2 all-gather.2

commit v2 on v0

v2 whole, which is shorter than its diff:
```python
import functools
import math

import jax
import jax.numpy as jnp
import ml_dtypes
import numpy as np
from jax import lax
from jax.experimental import pallas as pl
from jax.experimental.pallas import tpu as pltpu
from jax.sharding import PartitionSpec as P

PTS = 128
EQ = 128
DIRS = 16
RHS = 4
NEAR = 27
CAP = 16
REACH = 2
HB = 8
PAR_DEV = 4
BOX_DEV = 32
HALF_BOX = 16
WINDOW = 64
FEATURES = 16

wave_number = 3.0
smoothing = 0.0625
sphere_radius = 2.5
golden_turn = 2.399963229728653
four_pi = 12.566370614359172

TURNS = wave_number / (2.0 * math.pi)
SCALE = TURNS * TURNS
COS_TERMS = (0.99995979, -19.73104169, 64.67343118, -82.40355071, 45.64655728)
SIN_TERMS = (6.2830558, -41.33121431, 81.36681533, -74.47800473, 32.78140114)
AMPLITUDE = TURNS / four_pi

F32, BF16 = jnp.float32, jnp.bfloat16


def surface_features():
    ordinal = np.arange(EQ).astype(np.float32)
    height = np.float32(1.0) - (np.float32(2.0) * ordinal + np.float32(1.0)) / np.float32(EQ)
    radial = np.sqrt(np.float32(1.0) - height * height)
    angles = ordinal * np.float32(golden_turn)
    surface = np.float32(sphere_radius) * np.stack(
        [radial * np.cos(angles), radial * np.sin(angles), height]
    )
    surface = surface.astype(np.float64)

    def split(values):
        parts = []
        for _ in range(3):
            part = values.astype(ml_dtypes.bfloat16).astype(np.float64)
            parts.append(part)
            values = values - part
        return parts

    coords = [split(-2.0 * SCALE * surface[k]) for k in range(3)]
    square = split(SCALE * ((surface * surface).sum(0) + smoothing))
    one = np.ones(EQ)
    rows = [coords[k][i] for i in range(3) for k in range(3)] + [one] * 3 + square + [0.0 * one]
    return np.stack(rows).astype(ml_dtypes.bfloat16)


def split3(values):
    high = values.astype(BF16).astype(F32)
    rest = values - high
    middle = rest.astype(BF16).astype(F32)
    return [high, middle, rest - middle]


def horner(terms, z):
    total = z * (AMPLITUDE * terms[-1]) + AMPLITUDE * terms[-2]
    for term in terms[-3::-1]:
        total = total * z + AMPLITUDE * term
    return total


def wave(scaled):
    inverse = lax.rsqrt(scaled)
    phase = scaled * inverse
    phase = phase - jnp.round(phase)
    z = phase * phase
    real = inverse * horner(COS_TERMS, z)
    imag = (inverse * phase) * horner(SIN_TERMS, z)
    return real.astype(BF16), imag.astype(BF16)


def source_features(coords):
    square = SCALE * sum(c * c for c in coords)
    one = jnp.ones_like(square)
    return coords * 3 + split3(square) + [one, one, one, jnp.zeros_like(one)]


def target_features(coords):
    square = SCALE * (sum(c * c for c in coords) + smoothing)
    one = jnp.ones_like(square)
    parts = [split3(-2.0 * SCALE * c) for c in coords]
    rows = [parts[k][i] for i in range(3) for k in range(3)]
    return rows + [one, one, one] + split3(square) + [jnp.zeros_like(one)]


def dot(a, b):
    return jnp.dot(a, b, preferred_element_type=F32)


def dot_nt(a, b):
    return lax.dot_general(a, b, (((1,), (1,)), ((), ())), preferred_element_type=F32)


def rows_at(start, step, size=None):
    return pl.ds(pl.multiple_of(start, step), size or step)


def one_hot(condition):
    return jnp.where(condition, 1.0, 0.0).astype(BF16)


def iota(shape, dim):
    return lax.broadcasted_iota(jnp.int32, shape, dim)


def kernel(
    grid,
    points_ref,
    charges_ref,
    near_box_ref,
    near_code_ref,
    send_ref,
    slot_ref,
    slot_dir_ref,
    coarse_ref,
    coarse_dir_ref,
    leaf_hbm,
    coarse_hbm,
    up_hbm,
    down_hbm,
    surf_x_ref,
    surf_y_ref,
    out_ref,
    pos_ref,
    own_ref,
    dense_ref,
    feature_ref,
    source_ref,
    target_ref,
    leaf_ref,
    coarse_tab_ref,
    up_ref,
    down_ref,
    hot_ref,
    hot_near_ref,
    raised_ref,
    outgoing_ref,
    send_buf,
    send_near,
    recv_buf,
    parent_buf,
    weight_ref,
    coarse_weight_ref,
    cone_ref,
    coarse_cone_ref,
    child_ref,
    local_ref,
    left_ref,
    near_ref,
    far_x_ref,
    far_ref,
    table_sem,
    pair_send,
    pair_recv,
    halo_send,
    halo_recv,
    all_send,
    all_recv,
    close_send,
    close_recv,
    parent_send,
    parent_recv,
):
    nz, nx, ny = grid
    peers = nz * nx * ny
    blocks = peers // 8
    me = lax.axis_index("boxes")
    core = lax.axis_index("dirs")
    other = 1 - core

    def around(step):
        return lax.rem(me + step + peers, peers)

    def remote(src, dst, send_sem, recv_sem, box_to, core_to):
        return pltpu.make_async_remote_copy(
            src_ref=src,
            dst_ref=dst,
            send_sem=send_sem,
            recv_sem=recv_sem,
            device_id=(box_to, core_to),
            device_id_type=pl.DeviceIdType.MESH,
        )

    points = points_ref[...].astype(F32)
    pos_ref[core, pl.ds(HB, BOX_DEV), :] = jnp.concatenate(
        [points, jnp.zeros((BOX_DEV, 64), F32)], axis=1
    )
    for k in range(3):
        piece = points[:, k * 64 : k * 64 + 64]
        own_ref[k] = jnp.concatenate([piece, piece], axis=1)
    sign = jnp.where(iota((RHS, 128), 1) < 64, 1.0, -1.0)

    def weigh(j, carry):
        q = charges_ref[j].astype(F32)
        both = jnp.concatenate([q * sign, pltpu.roll(q, 64, 1)], axis=0)
        dense_ref[core, HB + j] = jnp.concatenate(
            [both, jnp.zeros_like(both)], axis=0
        ).astype(BF16)
        return carry

    lax.fori_loop(0, BOX_DEV, weigh, 0, unroll=4)

    pair_copies = [
        remote(
            pos_ref.at[core, pl.ds(HB, BOX_DEV)],
            pos_ref.at[core, pl.ds(HB, BOX_DEV)],
            pair_send.at[0],
            pair_recv.at[0],
            me,
            other,
        ),
        remote(
            dense_ref.at[core, pl.ds(HB, BOX_DEV)],
            dense_ref.at[core, pl.ds(HB, BOX_DEV)],
            pair_send.at[1],
            pair_recv.at[1],
            me,
            other,
        ),
        remote(leaf_hbm, leaf_ref.at[core], pair_send.at[2], pair_recv.at[2], me, other),
        remote(coarse_hbm, coarse_tab_ref.at[core], pair_send.at[3], pair_recv.at[3], me, other),
    ]
    pair_copies[0].start()
    pair_copies[1].start()
    halo_copies = []
    edge = BOX_DEV + HB
    for side, (first, step) in enumerate(((BOX_DEV, 1), (HB, -1))):
        halo_copies.append(
            remote(
                pos_ref.at[core, pl.ds(first, HB)],
                pos_ref.at[core, pl.ds(side * edge, HB)],
                halo_send.at[2 * side],
                halo_recv.at[core],
                around(step),
                side,
            )
        )
        halo_copies.append(
            remote(
                dense_ref.at[core, pl.ds(first, HB)],
                dense_ref.at[core, pl.ds(side * edge, HB)],
                halo_send.at[2 * side + 1],
                halo_recv.at[2 + core],
                around(step),
                side,
            )
        )
    for copy in halo_copies:
        copy.start()
    table_copies = [
        pltpu.make_async_copy(up_hbm, up_ref, table_sem.at[0]),
        pltpu.make_async_copy(coarse_hbm, coarse_tab_ref.at[core], table_sem.at[1]),
        pltpu.make_async_copy(down_hbm, down_ref, table_sem.at[2]),
        pltpu.make_async_copy(leaf_hbm, leaf_ref.at[core], table_sem.at[3]),
    ]
    for copy in table_copies:
        copy.start()
    pair_copies[2].start()
    pair_copies[3].start()

    slot_row = iota((16, CAP), 0)
    slot_lane = iota((16, CAP), 1)
    first_slots = slot_lane == slot_row % 8
    last_slots = slot_lane == slot_row % 8 + 8
    column = iota((16, 64), 1).astype(F32) - (32 * (iota((16, 64), 0) // 8)).astype(F32)

    def slots_of(t, mask):
        row = send_ref[pl.ds(t, 1), :].astype(F32)
        wanted = jnp.sum(jnp.where(mask, row, 0.0), axis=1, keepdims=True)
        return one_hot(wanted == column)

    def mark(t, carry):
        hot_ref[rows_at(t * 16, 16), :] = slots_of(t, first_slots)
        return carry

    lax.fori_loop(0, peers, mark, 0, unroll=8)
    for index in range(5):
        hot_near_ref[pl.ds(index * 16, 16), :] = slots_of(around(index - REACH), last_slots)
    recv_buf[pl.ds((peers + 5) * 16, 48), :] = jnp.zeros((48, 256), BF16)

    def features(first, count):
        coords = [
            jnp.concatenate(
                [
                    pos_ref[0, rows_at(first, HB, count), :][:, k * 64 : k * 64 + 64],
                    pos_ref[1, rows_at(first, HB, count), :][:, k * 64 : k * 64 + 64],
                ],
                axis=1,
            )
            for k in range(3)
        ]
        for f, row in enumerate(source_features(coords)):
            feature_ref[pl.ds(first * FEATURES + f, count, stride=FEATURES), :] = row

        def turn(i, carry):
            j = first + i
            tile = feature_ref[rows_at(j * FEATURES, FEATURES), :]
            source_ref[j] = tile.T.astype(BF16)
            return carry

        lax.fori_loop(0, count, turn, 0, unroll=4)

    pair_copies[0].wait_recv()
    features(HB, BOX_DEV)
    pair_copies[1].wait_recv()

    def charges_at(j):
        return jnp.concatenate([dense_ref[0, j], dense_ref[1, j]], axis=1)

    def kernel_tile(y, x):
        parts = []
        for half in range(2):
            parts.extend(wave(dot(y[half * 64 : half * 64 + 64], x)))
        return jnp.concatenate(parts, axis=0)

    surf_x = surf_x_ref[...]

    def raise_box(b, carry):
        tile = kernel_tile(source_ref[HB + b], surf_x)
        raised_ref[rows_at(b * 8, 8), :] = dot(charges_at(HB + b), tile)[:8]
        return carry

    lax.fori_loop(0, BOX_DEV, raise_box, 0, unroll=4)
    outgoing = []
    for r in range(2):
        pieces = [
            raised_ref[pl.ds(2 * core + r + 4 * part, BOX_DEV, stride=8), :] for part in range(2)
        ]
        outgoing.append(jnp.concatenate(pieces, axis=1).astype(BF16))
    outgoing = jnp.concatenate(outgoing, axis=0)
    outgoing_ref[0] = outgoing[:, :128].astype(F32)
    outgoing_ref[1] = outgoing[:, 128:].astype(F32)

    def fill(block, carry):
        rows = rows_at(block * 128, 128)
        send_buf[rows, :] = dot(hot_ref[rows, :], outgoing).astype(BF16)
        return carry

    lax.fori_loop(0, blocks, fill, 0, unroll=min(4, blocks))
    send_near[...] = dot(hot_near_ref[...], outgoing).astype(BF16)

    def leaf_copy(t):
        return remote(
            send_buf.at[rows_at(t * 16, 16)],
            recv_buf.at[rows_at(me * 16, 16)],
            all_send,
            all_recv,
            t,
            core,
        )

    table_copies[0].wait()
    parent = jnp.zeros((8, 256), F32)
    for o in range(8):
        pieces = [outgoing_ref[part, pl.ds(o, 8, stride=8), :] for part in range(2)]
        parent += dot(jnp.concatenate(pieces, axis=1).astype(BF16), up_ref[o])
    mz, mx, my = me // (nx * ny), me // ny % nx, me % ny
    mine = (my * nx + mx) * nz + mz
    parent_buf[rows_at(mine * 16, 16), :] = jnp.concatenate(
        [parent[:, :128], parent[:, 128:]], axis=0
    ).astype(BF16)

    def parent_phase(phase):
        count = (nz, nx, ny)[phase]
        size = (16, 16 * nz, 16 * nz * nx)[phase]
        rows = rows_at((mine * 16) // size * size, size)
        copies = []
        for step in range(1, count):
            if phase == 0:
                to = lax.rem(mz + step, nz) * nx * ny + mx * ny + my
            elif phase == 1:
                to = mz * nx * ny + lax.rem(mx + step, nx) * ny + my
            else:
                to = mz * nx * ny + mx * ny + lax.rem(my + step, ny)
            copies.append(
                remote(
                    parent_buf.at[rows],
                    parent_buf.at[rows],
                    parent_send.at[phase],
                    parent_recv.at[phase],
                    to,
                    core,
                )
            )
        every = pl.ds(0, size * (count - 1))
        total = remote(
            parent_buf.at[every],
            parent_buf.at[every],
            parent_send.at[phase],
            parent_recv.at[phase],
            me,
            other,
        )
        return copies, total

    phases = [parent_phase(phase) for phase in range(3)]
    for copy in phases[0][0]:
        copy.start()

    def send_leaf(step, carry):
        leaf_copy(around(step)).start()
        return carry

    close_copies = []
    for index, step in enumerate((-2, -1, 1, 2)):
        close_copies.append(
            remote(
                send_near.at[pl.ds((step + REACH) * 16, 16)],
                recv_buf.at[pl.ds((peers + REACH - step) * 16, 16)],
                close_send.at[index],
                close_recv.at[index],
                around(step),
                core,
            )
        )
    for copy in close_copies:
        copy.start()
    lax.fori_loop(1, peers, send_leaf, 0)
    recv_buf[rows_at(me * 16, 16), :] = send_buf[rows_at(me * 16, 16), :]
    recv_buf[pl.ds((peers + REACH) * 16, 16), :] = send_near[pl.ds(REACH * 16, 16), :]

    for half in range(2):
        remote(
            pos_ref.at[half, pl.ds(HB, HB)],
            pos_ref.at[half, rows_at(core * edge, HB)],
            halo_send.at[0],
            halo_recv.at[half],
            me,
            other,
        ).wait_recv()
        remote(
            dense_ref.at[half, pl.ds(HB, HB)],
            dense_ref.at[half, pl.ds(core * edge, HB)],
            halo_send.at[1],
            halo_recv.at[2 + half],
            me,
            other,
        ).wait_recv()
    features(core * edge, HB)
    first_box = core * HALF_BOX
    near_rows = rows_at(HB + first_box, HB, HALF_BOX)
    mine_coords = [
        jnp.concatenate(
            [
                pos_ref[0, near_rows, :][:, k * 64 : k * 64 + 64],
                pos_ref[1, near_rows, :][:, k * 64 : k * 64 + 64],
            ],
            axis=1,
        )
        for k in range(3)
    ]
    for code in range(27):
        offset = (2.0 * (code // 9 - 1), 2.0 * (code // 3 % 3 - 1), 2.0 * (code % 3 - 1))
        moved = [c - o for c, o in zip(mine_coords, offset)]
        for f, row in enumerate(target_features(moved)):
            far_x_ref[pl.ds(f, HALF_BOX, stride=FEATURES), :] = row
        for b in range(HALF_BOX):
            target_ref[code * HALF_BOX + b] = far_x_ref[pl.ds(b * FEATURES, FEATURES), :].astype(
                BF16
            )

    def near_box_sum(b, carry):
        def group(g, total):
            for i in range(9):
                n = g * 9 + i
                j = (near_box_ref[first_box + b, n] - me * BOX_DEV + HB) & (WINDOW - 1)
                code = near_code_ref[first_box + b, n]
                tile = kernel_tile(source_ref[j], target_ref[code * HALF_BOX + b])
                total = total + dot(charges_at(j), tile)
            return total

        total = lax.fori_loop(0, 3, group, jnp.zeros((16, PTS), F32))
        near_ref[rows_at((first_box + b) * 8, 8), :] = total[:8]
        return carry

    lax.fori_loop(0, 5, near_box_sum, 0)
    phases[0][1].wait_recv()
    for copy in phases[1][0]:
        copy.start()
    lax.fori_loop(5, 10, near_box_sum, 0)
    phases[1][1].wait_recv()
    for copy in phases[2][0]:
        copy.start()
    lax.fori_loop(10, HALF_BOX, near_box_sum, 0)
    near_copy = remote(
        near_ref.at[rows_at(core * 128, 128)],
        near_ref.at[rows_at(core * 128, 128)],
        pair_send.at[4],
        pair_recv.at[4],
        me,
        other,
    )
    near_copy.start()

    lane = iota((HALF_BOX, 128), 1)
    pair_coords = [
        jnp.where(
            lane < 64,
            own_ref[k, pl.ds(0, HALF_BOX, stride=2), :],
            own_ref[k, pl.ds(1, HALF_BOX, stride=2), :],
        )
        for k in range(3)
    ]
    for f, row in enumerate(source_features(pair_coords)):
        far_x_ref[pl.ds(f, HALF_BOX, stride=FEATURES), :] = row
    surf_y = surf_y_ref[...]

    def lower(pair, carry):
        x = far_x_ref[rows_at(pair * FEATURES, FEATURES), :].astype(BF16)
        real, imag = wave(dot(surf_y, x))
        far_ref[rows_at(pair * 256, 256), :] = jnp.concatenate([real, imag], axis=0)
        return carry

    lax.fori_loop(0, HALF_BOX, lower, 0, unroll=2)

    head = iota(((blocks + 1) * 16, 128), 0)
    tail = iota((256, 128), 0)
    tail = tail % 128 - 8 * (tail // 128)

    def count_slots(b, carry):
        v = slot_ref[pl.ds(b, 1), :]
        s, c = v >> 4, v & 15
        late = c >= 8
        gap = (s - me + REACH) & (peers - 1)
        high = jnp.where(late, blocks, s >> 3)
        low = jnp.where(late, gap * 16 + c - 8, (s & 7) * 16 + c)
        a = one_hot(head == high * 16 + slot_dir_ref[pl.ds(b, 1), :])
        counts = dot_nt(a, one_hot(tail == low)).astype(BF16)
        for h in range(blocks + 1):
            for r in range(2):
                weight_ref[r, rows_at(b * 16, 16), pl.ds(h * 128, 128)] = counts[
                    h * 16 : h * 16 + 16, r * 128 : r * 128 + 128
                ]
        return carry

    lax.fori_loop(0, BOX_DEV, count_slots, 0)

    coarse_head = iota((blocks * 16, 32), 0)
    coarse_tail = iota((512, 32), 0)
    coarse_tail = coarse_tail % 128 - 4 * (coarse_tail // 128)
    for p in range(PAR_DEV):
        v = coarse_ref[pl.ds(p, 1), :]
        dev, q = v >> 2, v & 3
        dz, dx, dy = dev >> ((nx * ny).bit_length() - 1), dev >> (ny.bit_length() - 1), dev
        place = ((dy & (ny - 1)) * nx + (dx & (nx - 1))) * nz + dz
        a = one_hot(coarse_head == (place >> 3) * 16 + coarse_dir_ref[pl.ds(p, 1), :])
        counts = dot_nt(a, one_hot(coarse_tail == (place & 7) * 16 + q)).astype(BF16)
        for h in range(blocks):
            for part in range(4):
                coarse_weight_ref[part, pl.ds(p * 16, 16), pl.ds(h * 128, 128)] = counts[
                    h * 16 : h * 16 + 16, part * 128 : part * 128 + 128
                ]
    phases[2][1].wait_recv()
    parents = parent_buf[...]
    for part in range(4):
        coarse_cone_ref[part // 2, pl.ds(part % 2 * 64, 64), :] = dot(
            coarse_weight_ref[part], parents
        )
    table_copies[1].wait()
    pair_copies[3].wait_recv()
    coarse_local = jnp.zeros((8, 256), F32)
    for d in range(DIRS):
        pieces = [coarse_cone_ref[part, pl.ds(d, 8, stride=16), :] for part in range(2)]
        coarse_local += dot(
            jnp.concatenate(pieces, axis=1).astype(BF16), coarse_tab_ref[d // 8, d % 8]
        )
    coarse_local = coarse_local.astype(BF16)
    table_copies[2].wait()
    for o in range(8):
        child = dot(coarse_local, down_ref[o])
        for part in range(2):
            child_ref[part, pl.ds(o, 8, stride=8), :] = child[:, part * 128 : part * 128 + 128]

    every = pl.ds(0, (peers - 1) * 16)
    all_copies = remote(send_buf.at[every], recv_buf.at[every], all_send, all_recv, me, other)
    all_copies.wait_recv()
    for copy in close_copies:
        copy.wait_recv()

    def leaf_cones(block, carry):
        rows = rows_at(block * 128, 128)
        received = recv_buf[...]
        for r in range(2):
            cone = dot(weight_ref[r, rows, :], received)
            to = rows_at(r * 512 + block * 128, 128)
            cone_ref[0, to, :] = cone[:, :128]
            cone_ref[1, to, :] = cone[:, 128:]
        return carry

    lax.fori_loop(0, 4, leaf_cones, 0)
    table_copies[3].wait()
    pair_copies[2].wait_recv()
    local = jnp.concatenate([child_ref[0], child_ref[1]], axis=1)
    for d in range(DIRS):
        pieces = [cone_ref[part, pl.ds(d, 64, stride=16), :] for part in range(2)]
        local += dot(jnp.concatenate(pieces, axis=1).astype(BF16), leaf_ref[d // 8, d % 8])
    local_ref[core] = local.astype(BF16)
    local_copy = remote(
        local_ref.at[core], local_ref.at[core], pair_send.at[5], pair_recv.at[5], me, other
    )
    local_copy.start()
    near_copy.wait_recv()
    local_copy.wait_recv()
    for half in range(2):
        for r in range(2):
            piece = local_ref[half, pl.ds(r * BOX_DEV, BOX_DEV), :].astype(F32)
            real, imag = piece[:, :128], piece[:, 128:]
            row = 2 * half + r
            left_ref[0, pl.ds(row, BOX_DEV, stride=8), :] = real
            left_ref[1, pl.ds(row, BOX_DEV, stride=8), :] = -imag
            left_ref[0, pl.ds(row + RHS, BOX_DEV, stride=8), :] = imag
            left_ref[1, pl.ds(row + RHS, BOX_DEV, stride=8), :] = real
    lane = iota((16, 128), 1)
    swap = (iota((16, 128), 0) < 8) == (core == 1)
    low_lane = iota((RHS, 128), 1) < 64

    def finish(pair, carry):
        rows = rows_at(pair * 16, 16)
        left = jnp.concatenate([left_ref[0, rows, :], left_ref[1, rows, :]], axis=1).astype(BF16)
        near = near_ref[rows, :]
        total = dot(left, far_ref[rows_at(pair * 256, 256), :]) + jnp.where(
            swap, pltpu.roll(near, 64, 1), near
        )
        turned = pltpu.roll(total, 64, 1)
        out_ref[2 * pair, 0] = jnp.where(low_lane, total[0:4], turned[4:8]).astype(BF16)
        out_ref[2 * pair + 1, 0] = jnp.where(low_lane, turned[8:12], total[12:16]).astype(BF16)
        return carry

    lax.fori_loop(0, HALF_BOX, finish, 0, unroll=2)

    for copy in pair_copies + halo_copies + close_copies + [near_copy, local_copy]:
        copy.wait_send()
    all_copies.wait_send()
    for phase in range(3):
        phases[phase][1].wait_send()


def on_device(
    grid,
    points,
    charges,
    near_box,
    near_code,
    send_box,
    far_slot,
    far_direction,
    coarse_source,
    coarse_direction,
    leaf_translate,
    coarse_translate,
    child_to_parent,
    parent_to_child,
):
    peers = grid[0] * grid[1] * grid[2]
    blocks = peers // 8
    vmem = pl.BlockSpec(memory_space=pltpu.VMEM)
    smem = pl.BlockSpec(memory_space=pltpu.SMEM)
    hbm = pl.BlockSpec(memory_space=pl.ANY)
    surf = surface_features()
    dma = pltpu.SemaphoreType.DMA
    return pl.pallas_call(
        functools.partial(kernel, grid),
        out_shape=jax.ShapeDtypeStruct((BOX_DEV, 1, RHS, 128), BF16),
        in_specs=[vmem, vmem, smem, smem, vmem, vmem, vmem, vmem, vmem]
        + [hbm, hbm, hbm, hbm, vmem, vmem],
        out_specs=vmem,
        scratch_shapes=[
            pltpu.VMEM((2, WINDOW, 256), F32),
            pltpu.VMEM((3, BOX_DEV, 128), F32),
            pltpu.VMEM((2, WINDOW, 16, 128), BF16),
            pltpu.VMEM((WINDOW * FEATURES, 128), F32),
            pltpu.VMEM((WINDOW, PTS, FEATURES), BF16),
            pltpu.VMEM((27 * HALF_BOX, FEATURES, 128), BF16),
            pltpu.VMEM((2, 8, 256, 256), BF16),
            pltpu.VMEM((2, 8, 256, 256), BF16),
            pltpu.VMEM((8, 256, 256), BF16),
            pltpu.VMEM((8, 256, 256), BF16),
            pltpu.VMEM((peers * 16, 64), BF16),
            pltpu.VMEM((5 * 16, 64), BF16),
            pltpu.VMEM((BOX_DEV * 8, 128), F32),
            pltpu.VMEM((2, 64, 128), F32),
            pltpu.VMEM((peers * 16, 256), BF16),
            pltpu.VMEM((5 * 16, 256), BF16),
            pltpu.VMEM(((peers + 8) * 16, 256), BF16),
            pltpu.VMEM((peers * 16, 128), BF16),
            pltpu.VMEM((2, BOX_DEV * DIRS, (blocks + 1) * 128), BF16),
            pltpu.VMEM((4, PAR_DEV * DIRS, blocks * 128), BF16),
            pltpu.VMEM((2, 2 * BOX_DEV * DIRS, 128), F32),
            pltpu.VMEM((2, 2 * PAR_DEV * DIRS, 128), F32),
            pltpu.VMEM((2, 64, 128), F32),
            pltpu.VMEM((2, 64, 256), BF16),
            pltpu.VMEM((2, BOX_DEV * 8, 128), F32),
            pltpu.VMEM((BOX_DEV * 8, 128), F32),
            pltpu.VMEM((HALF_BOX * FEATURES, 128), F32),
            pltpu.VMEM((HALF_BOX * 256, 128), BF16),
            dma((4,)),
            dma((6,)),
            dma((6,)),
            dma((4,)),
            dma((4,)),
            dma,
            dma,
            dma((4,)),
            dma((4,)),
            dma((3,)),
            dma((3,)),
        ],
        compiler_params=pltpu.CompilerParams(
            has_side_effects=True, vmem_limit_bytes=48 * 1024 * 1024
        ),
        cost_estimate=pl.CostEstimate(
            flops=5 * 10**9, bytes_accessed=10**7, transcendentals=10**7
        ),
        name="multipole",
    )(
        points[:, 0],
        charges[:, 0],
        near_box,
        near_code,
        send_box,
        far_slot,
        far_direction,
        coarse_source,
        coarse_direction,
        leaf_translate,
        coarse_translate,
        child_to_parent,
        parent_to_child,
        jnp.asarray(surf),
        jnp.asarray(np.ascontiguousarray(surf.T)),
    )


def solution(mesh):
    peers = mesh.shape["boxes"]
    grid = {128: (8, 4, 4), 8: (2, 2, 2)}[peers]
    return jax.shard_map(
        functools.partial(on_device, grid),
        mesh=mesh,
        in_specs=(
            P("boxes", "dirs", None),
            P("boxes", "dirs", None, None),
            P("boxes", None),
            P("boxes", None),
            P("boxes", None),
            P("boxes", None),
            P("boxes", None),
            P("boxes", None),
            P("boxes", None),
            P("dirs", None, None),
            P("dirs", None, None),
            P(),
            P(),
        ),
        out_specs=P("boxes", "dirs", None, None),
        check_vma=False,
    )
```

time: 676 us -> 90 us (0.13)
  blocking collectives: 358 us -> 0 us
  other arithmetic: 142 us -> 0 us
  local copies, waits for them, and re-layouts: 102 us -> 9.29 us
  Pallas kernels: 0 us -> 80.1 us
  matrix products: 30.1 us -> 0 us
  starting transfers between devices: 25.5 us -> 0 us
  between operations: 13.8 us -> 0.1 us
    all_gather x4 -> x0, blocking collectives: 358 us -> none  [the longest x1 292 us: on_device(): shard_rows = lax.all_gather(parent, 'boxes', axis=0, tiled=True)]
    convert_element_type x5 -> x0, other arithmetic: 117 us -> none  [the longest x4 113 us: kernel_parts(): (amplitude * jnp.sin(wave_number * spread)).astype(jnp.bfloat16)]
    pallas_call x0 -> x1, Pallas kernels: none -> 80.1 us  [on_device(): pl.pallas_call(functools.partial(kernel, grid), out_shape=jax.ShapeDtypeS...]
    gather x3 -> x0, local copies, waits for them, and re-layouts: 42.4 us -> none  [the longest x1 17.3 us: on_device(): gathered = arrived.reshape(peer_count * CAP, rhs_half * 2 * EQ)[far_slot]]
    dot_general x30 -> x0, matrix products: 30.1 us -> none  [the longest x16 17.2 us: near_contract(): jnp.einsum('gkps,gkrs->grp', kern, charge, preferred_element_type=jnp.flo...]
    while x6 -> x0, local copies, waits for them, and re-layouts: 25.7 us -> none  [on_device(): lax.map(near_group, (my_pos.reshape(groups, 8, 3, half_pts), source_pos.r...]
    all_to_all x1 -> x0, starting transfers between devices: 19.7 us -> none  [on_device(): lax.all_to_all(outbound, 'boxes', split_axis=0, concat_axis=0, tiled=True)]
    slice x5 -> x0, local copies, waits for them, and re-layouts: 16.8 us -> none  [the longest x1 8.59 us: on_device(): source_charge[:, :, :, :, 1, :]]
  transfers between devices with their start and end apart: 6 -> 0, of which waited for: 0 -> 0; matrix products, arithmetic and copies ran while one was open for 39% -> 0% of each run, Pallas kernels for 0% -> 0%
where the time goes in v2:
time: 90 us; the launch traced here: 89.5 us
  Pallas kernels  80.1 us (89%)
  local copies, waits for them, and re-layouts  9.29 us (10%)
    pallas_call x1, Pallas kernels, on_device(): pl.pallas_call(functools.partial(kernel, grid), out_shape=jax.ShapeDtypeS...  80.1 us
    unnamed x30, local copies, waits for them, and re-layouts  9.29 us

profile of v2, /device:TPU:1, one launch (start us, length us, event | category | flops | bytes accessed | tf_op | source)
XLA Modules:
  0.0 89.5 jit_solution(2793683662988221011)
XLA Ops:
  0.0 0.0 copy-start.4
  0.0 0.0 copy-start.5
  0.0 0.0 copy-start.6
  0.0 0.0 copy-start.10
  0.0 0.0 copy-start.11
  0.0 0.0 copy-start.13
  0.0 0.8 copy.16.send_ref
  0.9 0.0 copy-done.4
  0.9 0.0 copy-done.5
  0.9 0.0 copy-done.6
  0.9 0.0 copy-done.10
  0.9 0.0 copy-done.11
  0.9 0.0 copy-done.13
  0.9 0.0 copy-start
  1.0 1.2 %copy-done = bf16[8,256,256]{2,1,0:T(8,128)(2,1)S(1)} copy-done((bf16[8,256,256]{2,1,0:T(8,128)(2,1)S(1)}, bf16[8,256,256]{2,1,0:T(8,128)(2,1)}, u32[]{:S(2)}) %copy-start) | copy-done | bytes 1048600
  2.2 0.0 copy-start.1
  2.2 1.2 %copy-done.1 = bf16[8,256,256]{2,1,0:T(8,128)(2,1)S(1)} copy-done((bf16[8,256,256]{2,1,0:T(8,128)(2,1)S(1)}, bf16[8,256,256]{2,1,0:T(8,128)(2,1)}, u32[]{:S(2)}) %copy-start.1) | copy-done | bytes 1048600
  3.4 0.0 copy-start.2
  3.4 1.2 %copy-done.2 = bf16[8,256,256]{2,1,0:T(8,128)(2,1)S(1)} copy-done((bf16[8,256,256]{2,1,0:T(8,128)(2,1)S(1)}, bf16[8,256,256]{2,1,0:T(8,128)(2,1)}, u32[]{:S(2)}) %copy-start.2) | copy-done | bytes 1048600
  4.6 0.0 copy-start.3
  4.6 1.2 %copy-done.3 = bf16[8,256,256]{2,1,0:T(8,128)(2,1)S(1)} copy-done((bf16[8,256,256]{2,1,0:T(8,128)(2,1)S(1)}, bf16[8,256,256]{2,1,0:T(8,128)(2,1)}, u32[]{:S(2)}) %copy-start.3) | copy-done | bytes 1048600
  5.9 0.0 copy-start.7
  5.9 0.7 copy-done.7
  6.6 0.0 copy-start.8
  6.6 0.7 copy-done.8
  7.3 0.0 copy-start.9
  7.3 0.7 copy-done.9
  8.0 0.0 copy-start.12
  8.0 0.8 copy-done.12
  8.8 80.1 %multipole.1 = bf16[32,1,4,128]{3,2,1,0:T(4,128)(2,1)S(1)} custom-call(bf16[32,192]{1,0:T(8,128)(2,1)S(1)} %bitcast.3, bf16[32,4,128]{2,1,0:T(4,128)(2,1)S(1)} %bitcast.2, s32[32,27]{1,0:T(8,128)S(1)} %copy-done.6, s32[32,27]{1,0:T(8,128)S(1)} %copy-done.7, s32[128,16]{1,0:T(8,128)S(1)} %copy.16.send_ref, s32[32,128]{1,0:T(8,128)S(1)} %copy-done.8, ...), custom_call_target="tpu_custom_call" | custom-call | flops 5000000000 | bytes 10000000 | tf_op jit(solution)/shard_map/multipole/pallas_call | solution.py:680
  88.9 0.6 copy.18
Async XLA Ops:
  0.0 0.9 copy-start.4
  0.0 0.9 %copy-start.5 = (bf16[32,1,192]{2,0,1:T(8,128)(2,1)S(1)}, bf16[32,1,192]{2,0,1:T(8,128)(2,1)}, u32[]{:S(2)}) copy-start(bf16[32,1,192]{2,0,1:T(8,128)(2,1)} %param.15) | copy-start | bytes 36868
  0.0 0.9 %copy-start.6 = (s32[32,27]{1,0:T(8,128)S(1)}, s32[32,27]{1,0:T(8,128)}, u32[]{:S(2)}) copy-start(s32[32,27]{1,0:T(8,128)} %near_box_ref.1) | copy-start | bytes 10372
  0.0 0.9 %copy-start.10 = (s32[4,32]{1,0:T(4,128)S(1)}, s32[4,32]{1,0:T(4,128)}, u32[]{:S(2)}) copy-start(s32[4,32]{1,0:T(4,128)} %coarse_ref.1) | copy-start | bytes 1540
  0.0 0.9 %copy-start.11 = (s32[4,32]{1,0:T(4,128)S(1)}, s32[4,32]{1,0:T(4,128)}, u32[]{:S(2)}) copy-start(s32[4,32]{1,0:T(4,128)} %coarse_dir_ref.1) | copy-start | bytes 1540
  0.0 0.9 %copy-start.13 = (bf16[16,128]{1,0:T(8,128)(2,1)S(1)}, bf16[16,128]{1,0:T(8,128)(2,1)}, u32[]{:S(2)}) copy-start(bf16[16,128]{1,0:T(8,128)(2,1)} %constant.4.clone.surf_x_ref) | copy-start | bytes 12292
  0.9 1.2 %copy-start = (bf16[8,256,256]{2,1,0:T(8,128)(2,1)S(1)}, bf16[8,256,256]{2,1,0:T(8,128)(2,1)}, u32[]{:S(2)}) copy-start(bf16[8,256,256]{2,1,0:T(8,128)(2,1)} %leaf_hbm.1) | copy-start | bytes 3145732
  2.2 1.2 %copy-start.1 = (bf16[8,256,256]{2,1,0:T(8,128)(2,1)S(1)}, bf16[8,256,256]{2,1,0:T(8,128)(2,1)}, u32[]{:S(2)}) copy-start(bf16[8,256,256]{2,1,0:T(8,128)(2,1)} %coarse_hbm.1) | copy-start | bytes 3145732
  3.4 1.2 %copy-start.2 = (bf16[8,256,256]{2,1,0:T(8,128)(2,1)S(1)}, bf16[8,256,256]{2,1,0:T(8,128)(2,1)}, u32[]{:S(2)}) copy-start(bf16[8,256,256]{2,1,0:T(8,128)(2,1)} %up_hbm.1) | copy-start | bytes 3145732
  4.6 1.2 %copy-start.3 = (bf16[8,256,256]{2,1,0:T(8,128)(2,1)S(1)}, bf16[8,256,256]{2,1,0:T(8,128)(2,1)}, u32[]{:S(2)}) copy-start(bf16[8,256,256]{2,1,0:T(8,128)(2,1)} %down_hbm.1) | copy-start | bytes 3145732
  5.9 0.7 copy-start.7
  6.6 0.7 copy-start.8
  7.3 0.7 copy-start.9
  8.0 0.8 copy-start.12

commit v3 on v2

--- a/solution.py
+++ b/solution.py
@@ -36,6 +36,7 @@
 SIN_TERMS = (6.2830558, -41.33121431, 81.36681533, -74.47800473, 32.78140114)
 AMPLITUDE = TURNS / four_pi
 
+VMEM_BYTES = 62 * 1024 * 1024
 F32, BF16 = jnp.float32, jnp.bfloat16
 
 
@@ -128,11 +129,11 @@
     charges_ref,
     near_box_ref,
     near_code_ref,
-    send_ref,
-    slot_ref,
-    slot_dir_ref,
-    coarse_ref,
-    coarse_dir_ref,
+    send_hbm,
+    slot_hbm,
+    slot_dir_hbm,
+    coarse_source_hbm,
+    coarse_dir_hbm,
     leaf_hbm,
     coarse_hbm,
     up_hbm,
@@ -168,7 +169,13 @@
     near_ref,
     far_x_ref,
     far_ref,
+    send_ref,
+    slot_ref,
+    slot_dir_ref,
+    coarse_ref,
+    coarse_dir_ref,
     table_sem,
+    list_sem,
     pair_send,
     pair_recv,
     halo_send,
@@ -200,6 +207,21 @@
             device_id_type=pl.DeviceIdType.MESH,
         )
 
+    list_copies = [
+        pltpu.make_async_copy(src, dst, list_sem.at[i])
+        for i, (src, dst) in enumerate(
+            (
+                (send_hbm, send_ref),
+                (slot_hbm, slot_ref),
+                (slot_dir_hbm, slot_dir_ref),
+                (coarse_source_hbm, coarse_ref),
+                (coarse_dir_hbm, coarse_dir_ref),
+            )
+        )
+    ]
+    for copy in list_copies:
+        copy.start()
+
     points = points_ref[...].astype(F32)
     pos_ref[core, pl.ds(HB, BOX_DEV), :] = jnp.concatenate(
         [points, jnp.zeros((BOX_DEV, 64), F32)], axis=1
@@ -212,9 +234,7 @@
     def weigh(j, carry):
         q = charges_ref[j].astype(F32)
         both = jnp.concatenate([q * sign, pltpu.roll(q, 64, 1)], axis=0)
-        dense_ref[core, HB + j] = jnp.concatenate(
-            [both, jnp.zeros_like(both)], axis=0
-        ).astype(BF16)
+        dense_ref[core, HB + j] = jnp.concatenate([both, both], axis=0).astype(BF16)
         return carry
 
     lax.fori_loop(0, BOX_DEV, weigh, 0, unroll=4)
@@ -277,6 +297,7 @@
     pair_copies[2].start()
     pair_copies[3].start()
 
+    list_copies[0].wait()
     slot_row = iota((16, CAP), 0)
     slot_lane = iota((16, CAP), 1)
     first_slots = slot_lane == slot_row % 8
@@ -314,7 +335,10 @@
         def turn(i, carry):
             j = first + i
             tile = feature_ref[rows_at(j * FEATURES, FEATURES), :]
-            source_ref[j] = tile.T.astype(BF16)
+            turned = tile.T
+            blank = jnp.zeros_like(turned)
+            source_ref[0, j] = jnp.concatenate([turned, blank], axis=1).astype(BF16)
+            source_ref[1, j] = jnp.concatenate([blank, turned], axis=1).astype(BF16)
             return carry
 
         lax.fori_loop(0, count, turn, 0, unroll=4)
@@ -329,13 +353,14 @@
     def kernel_tile(y, x):
         parts = []
         for half in range(2):
-            parts.extend(wave(dot(y[half * 64 : half * 64 + 64], x)))
+            pieces = [wave(dot(y[at : at + 32], x)) for at in (half * 64, half * 64 + 32)]
+            parts.extend([piece[0] for piece in pieces] + [piece[1] for piece in pieces])
         return jnp.concatenate(parts, axis=0)
 
     surf_x = surf_x_ref[...]
 
     def raise_box(b, carry):
-        tile = kernel_tile(source_ref[HB + b], surf_x)
+        tile = kernel_tile(source_ref[0, HB + b][:, :FEATURES], surf_x)
         raised_ref[rows_at(b * 8, 8), :] = dot(charges_at(HB + b), tile)[:8]
         return carry
 
@@ -478,29 +503,47 @@
                 BF16
             )
 
-    def near_box_sum(b, carry):
+    upper = iota((16, 256), 0) < 8
+    pad = jnp.zeros((FEATURES, PTS), BF16)
+
+    def near_pair_sum(pair, carry):
+        b = 2 * pair
+
         def group(g, total):
             for i in range(9):
                 n = g * 9 + i
-                j = (near_box_ref[first_box + b, n] - me * BOX_DEV + HB) & (WINDOW - 1)
-                code = near_code_ref[first_box + b, n]
-                tile = kernel_tile(source_ref[j], target_ref[code * HALF_BOX + b])
-                total = total + dot(charges_at(j), tile)
+                j, code = [], []
+                for k in range(2):
+                    place = near_box_ref[first_box + b + k, n] - me * BOX_DEV + HB
+                    j.append(place & (WINDOW - 1))
+                    code.append(near_code_ref[first_box + b + k, n] * HALF_BOX + b + k)
+                y = source_ref[0, j[0]] + source_ref[1, j[1]]
+                x = jnp.concatenate(
+                    [
+                        jnp.concatenate([target_ref[code[0]], pad], axis=1),
+                        jnp.concatenate([pad, target_ref[code[1]]], axis=1),
+                    ],
+                    axis=0,
+                )
+                q = jnp.where(upper, charges_at(j[0]), charges_at(j[1]))
+                total = total + dot(q, kernel_tile(y, x))
             return total
 
-        total = lax.fori_loop(0, 3, group, jnp.zeros((16, PTS), F32))
-        near_ref[rows_at((first_box + b) * 8, 8), :] = total[:8]
-        return carry
-
-    lax.fori_loop(0, 5, near_box_sum, 0)
+        total = lax.fori_loop(0, 3, group, jnp.zeros((16, 2 * PTS), F32))
+        near_ref[rows_at((first_box + b) * 8, 16), :] = jnp.concatenate(
+            [total[:8, :PTS], total[8:, PTS:]], axis=0
+        )
+        return carry
+
+    lax.fori_loop(0, 2, near_pair_sum, 0)
     phases[0][1].wait_recv()
     for copy in phases[1][0]:
         copy.start()
-    lax.fori_loop(5, 10, near_box_sum, 0)
+    lax.fori_loop(2, 5, near_pair_sum, 0)
     phases[1][1].wait_recv()
     for copy in phases[2][0]:
         copy.start()
-    lax.fori_loop(10, HALF_BOX, near_box_sum, 0)
+    lax.fori_loop(5, HALF_BOX // 2, near_pair_sum, 0)
     near_copy = remote(
         near_ref.at[rows_at(core * 128, 128)],
         near_ref.at[rows_at(core * 128, 128)],
@@ -532,6 +575,8 @@
 
     lax.fori_loop(0, HALF_BOX, lower, 0, unroll=2)
 
+    for copy in list_copies[1:]:
+        copy.wait()
     head = iota(((blocks + 1) * 16, 128), 0)
     tail = iota((256, 128), 0)
     tail = tail % 128 - 8 * (tail // 128)
@@ -680,15 +725,14 @@
     return pl.pallas_call(
         functools.partial(kernel, grid),
         out_shape=jax.ShapeDtypeStruct((BOX_DEV, 1, RHS, 128), BF16),
-        in_specs=[vmem, vmem, smem, smem, vmem, vmem, vmem, vmem, vmem]
-        + [hbm, hbm, hbm, hbm, vmem, vmem],
+        in_specs=[vmem, vmem, smem, smem] + [hbm] * 9 + [vmem, vmem],
         out_specs=vmem,
         scratch_shapes=[
             pltpu.VMEM((2, WINDOW, 256), F32),
             pltpu.VMEM((3, BOX_DEV, 128), F32),
             pltpu.VMEM((2, WINDOW, 16, 128), BF16),
             pltpu.VMEM((WINDOW * FEATURES, 128), F32),
-            pltpu.VMEM((WINDOW, PTS, FEATURES), BF16),
+            pltpu.VMEM((2, WINDOW, PTS, 2 * FEATURES), BF16),
             pltpu.VMEM((27 * HALF_BOX, FEATURES, 128), BF16),
             pltpu.VMEM((2, 8, 256, 256), BF16),
             pltpu.VMEM((2, 8, 256, 256), BF16),
@@ -712,7 +756,13 @@
             pltpu.VMEM((BOX_DEV * 8, 128), F32),
             pltpu.VMEM((HALF_BOX * FEATURES, 128), F32),
             pltpu.VMEM((HALF_BOX * 256, 128), BF16),
+            pltpu.VMEM((peers, CAP), jnp.int32),
+            pltpu.VMEM((BOX_DEV, 128), jnp.int32),
+            pltpu.VMEM((BOX_DEV, 128), jnp.int32),
+            pltpu.VMEM((PAR_DEV, 32), jnp.int32),
+            pltpu.VMEM((PAR_DEV, 32), jnp.int32),
             dma((4,)),
+            dma((5,)),
             dma((6,)),
             dma((6,)),
             dma((4,)),
@@ -725,7 +775,7 @@
             dma((3,)),
         ],
         compiler_params=pltpu.CompilerParams(
-            has_side_effects=True, vmem_limit_bytes=48 * 1024 * 1024
+            has_side_effects=True, vmem_limit_bytes=VMEM_BYTES
         ),
         cost_estimate=pl.CostEstimate(
             flops=5 * 10**9, bytes_accessed=10**7, transcendentals=10**7

time: 90 us -> 79.2 us (0.88)
  local copies, waits for them, and re-layouts: 9.29 us -> 2.8 us
  Pallas kernels: 80.1 us -> 76 us
    unnamed x30 -> x2, local copies, waits for them, and re-layouts: 9.29 us -> 2.8 us
    pallas_call x1, Pallas kernels: 80.1 us -> 76 us  [on_device(): pl.pallas_call(functools.partial(kernel, grid), out_shape=jax.ShapeDtypeS...]
where the time goes in v3:
time: 79.2 us; the launch traced here: 78.9 us
  Pallas kernels  76 us (96%)
  local copies, waits for them, and re-layouts  2.8 us (4%)
    pallas_call x1, Pallas kernels, on_device(): pl.pallas_call(functools.partial(kernel, grid), out_shape=jax.ShapeDtypeS...  76 us
    unnamed x2, local copies, waits for them, and re-layouts  2.8 us

profile of v3, /device:TPU:1, one launch (start us, length us, event | category | flops | bytes accessed | tf_op | source)
XLA Modules:
  0.0 78.9 jit_solution(11945141514962036267)
XLA Ops:
  0.0 1.4 %copy.16.send_hbm = s32[128,16]{1,0:T(8,128)} copy(s32[128,16]{0,1:T(8,128)} %param.19) | data formatting | bytes 16384 | tf_op args[4]
  1.4 76.0 %multipole.1 = bf16[32,1,4,128]{3,2,1,0:T(4,128)(2,1)} custom-call(bf16[32,192]{1,0:T(8,128)(2,1)} %bitcast.3, bf16[32,4,128]{2,1,0:T(4,128)(2,1)} %bitcast.2, s32[32,27]{1,0:T(8,128)} %near_box_ref.1, s32[32,27]{1,0:T(8,128)} %near_code_ref.1, s32[128,16]{1,0:T(8,128)} %copy.16.send_hbm, s32[32,128]{1,0:T(8,128)} %slot_hbm.1, s32[32,128]{1,0:T(8,128)} %slot_dir_hbm.1, ...), custom_call_target="tpu_custom_call" | custom-call | flops 5000000000 | bytes 10000000 | tf_op jit(solution)/shard_map/multipole/pallas_call | solution.py:725
  77.5 1.4 %copy.18 = bf16[32,1,4,128]{3,2,1,0:T(4,128)(2,1)} copy(bf16[32,1,4,128]{3,2,1,0:T(4,128)(2,1)} %multipole.1) | data formatting | bytes 65536

commit v4 on v3

--- a/solution.py
+++ b/solution.py
@@ -170,6 +170,7 @@
     far_x_ref,
     far_ref,
     send_ref,
+    send_rows_ref,
     slot_ref,
     slot_dir_ref,
     coarse_ref,
@@ -237,7 +238,7 @@
         dense_ref[core, HB + j] = jnp.concatenate([both, both], axis=0).astype(BF16)
         return carry
 
-    lax.fori_loop(0, BOX_DEV, weigh, 0, unroll=4)
+    lax.fori_loop(0, BOX_DEV, weigh, 0, unroll=8)
 
     pair_copies = [
         remote(
@@ -298,6 +299,7 @@
     pair_copies[3].start()
 
     list_copies[0].wait()
+    send_rows_ref[...] = send_ref[...].astype(F32).T
     slot_row = iota((16, CAP), 0)
     slot_lane = iota((16, CAP), 1)
     first_slots = slot_lane == slot_row % 8
@@ -305,7 +307,7 @@
     column = iota((16, 64), 1).astype(F32) - (32 * (iota((16, 64), 0) // 8)).astype(F32)
 
     def slots_of(t, mask):
-        row = send_ref[pl.ds(t, 1), :].astype(F32)
+        row = send_rows_ref[pl.ds(t, 1), :]
         wanted = jnp.sum(jnp.where(mask, row, 0.0), axis=1, keepdims=True)
         return one_hot(wanted == column)
 
@@ -341,7 +343,7 @@
             source_ref[1, j] = jnp.concatenate([blank, turned], axis=1).astype(BF16)
             return carry
 
-        lax.fori_loop(0, count, turn, 0, unroll=4)
+        lax.fori_loop(0, count, turn, 0, unroll=8)
 
     pair_copies[0].wait_recv()
     features(HB, BOX_DEV)
@@ -364,7 +366,7 @@
         raised_ref[rows_at(b * 8, 8), :] = dot(charges_at(HB + b), tile)[:8]
         return carry
 
-    lax.fori_loop(0, BOX_DEV, raise_box, 0, unroll=4)
+    lax.fori_loop(0, BOX_DEV, raise_box, 0, unroll=8)
     outgoing = []
     for r in range(2):
         pieces = [
@@ -509,41 +511,41 @@
     def near_pair_sum(pair, carry):
         b = 2 * pair
 
-        def group(g, total):
-            for i in range(9):
-                n = g * 9 + i
-                j, code = [], []
-                for k in range(2):
-                    place = near_box_ref[first_box + b + k, n] - me * BOX_DEV + HB
-                    j.append(place & (WINDOW - 1))
-                    code.append(near_code_ref[first_box + b + k, n] * HALF_BOX + b + k)
-                y = source_ref[0, j[0]] + source_ref[1, j[1]]
-                x = jnp.concatenate(
-                    [
-                        jnp.concatenate([target_ref[code[0]], pad], axis=1),
-                        jnp.concatenate([pad, target_ref[code[1]]], axis=1),
-                    ],
-                    axis=0,
-                )
-                q = jnp.where(upper, charges_at(j[0]), charges_at(j[1]))
-                total = total + dot(q, kernel_tile(y, x))
-            return total
-
-        total = lax.fori_loop(0, 3, group, jnp.zeros((16, 2 * PTS), F32))
+        @pl.when(pair == 2)
+        def _():
+            phases[0][1].wait_recv()
+            for copy in phases[1][0]:
+                copy.start()
+
+        @pl.when(pair == 4)
+        def _():
+            phases[1][1].wait_recv()
+            for copy in phases[2][0]:
+                copy.start()
+
+        total = jnp.zeros((16, 2 * PTS), F32)
+        for n in range(NEAR):
+            j, code = [], []
+            for k in range(2):
+                place = near_box_ref[first_box + b + k, n] - me * BOX_DEV + HB
+                j.append(place & (WINDOW - 1))
+                code.append(near_code_ref[first_box + b + k, n] * HALF_BOX + b + k)
+            y = source_ref[0, j[0]] + source_ref[1, j[1]]
+            x = jnp.concatenate(
+                [
+                    jnp.concatenate([target_ref[code[0]], pad], axis=1),
+                    jnp.concatenate([pad, target_ref[code[1]]], axis=1),
+                ],
+                axis=0,
+            )
+            q = jnp.where(upper, charges_at(j[0]), charges_at(j[1]))
+            total = total + dot(q, kernel_tile(y, x))
         near_ref[rows_at((first_box + b) * 8, 16), :] = jnp.concatenate(
             [total[:8, :PTS], total[8:, PTS:]], axis=0
         )
         return carry
 
-    lax.fori_loop(0, 2, near_pair_sum, 0)
-    phases[0][1].wait_recv()
-    for copy in phases[1][0]:
-        copy.start()
-    lax.fori_loop(2, 5, near_pair_sum, 0)
-    phases[1][1].wait_recv()
-    for copy in phases[2][0]:
-        copy.start()
-    lax.fori_loop(5, HALF_BOX // 2, near_pair_sum, 0)
+    lax.fori_loop(0, HALF_BOX // 2, near_pair_sum, 0)
     near_copy = remote(
         near_ref.at[rows_at(core * 128, 128)],
         near_ref.at[rows_at(core * 128, 128)],
@@ -573,7 +575,7 @@
         far_ref[rows_at(pair * 256, 256), :] = jnp.concatenate([real, imag], axis=0)
         return carry
 
-    lax.fori_loop(0, HALF_BOX, lower, 0, unroll=2)
+    lax.fori_loop(0, HALF_BOX, lower, 0, unroll=8)
 
     for copy in list_copies[1:]:
         copy.wait()
@@ -597,7 +599,7 @@
                 ]
         return carry
 
-    lax.fori_loop(0, BOX_DEV, count_slots, 0)
+    lax.fori_loop(0, BOX_DEV, count_slots, 0, unroll=4)
 
     coarse_head = iota((blocks * 16, 32), 0)
     coarse_tail = iota((512, 32), 0)
@@ -690,7 +692,7 @@
         out_ref[2 * pair + 1, 0] = jnp.where(low_lane, turned[8:12], total[12:16]).astype(BF16)
         return carry
 
-    lax.fori_loop(0, HALF_BOX, finish, 0, unroll=2)
+    lax.fori_loop(0, HALF_BOX, finish, 0, unroll=8)
 
     for copy in pair_copies + halo_copies + close_copies + [near_copy, local_copy]:
         copy.wait_send()
@@ -756,7 +758,8 @@
             pltpu.VMEM((BOX_DEV * 8, 128), F32),
             pltpu.VMEM((HALF_BOX * FEATURES, 128), F32),
             pltpu.VMEM((HALF_BOX * 256, 128), BF16),
-            pltpu.VMEM((peers, CAP), jnp.int32),
+            pltpu.VMEM((CAP, peers), jnp.int32),
+            pltpu.VMEM((peers, CAP), F32),
             pltpu.VMEM((BOX_DEV, 128), jnp.int32),
             pltpu.VMEM((BOX_DEV, 128), jnp.int32),
             pltpu.VMEM((PAR_DEV, 32), jnp.int32),
@@ -786,7 +789,7 @@
         charges[:, 0],
         near_box,
         near_code,
-        send_box,
+        send_box.T,
         far_slot,
         far_direction,
         coarse_source,

time: 79.2 us -> 67.7 us (0.85)
  Pallas kernels: 76 us -> 66.1 us
  local copies, waits for them, and re-layouts: 2.8 us -> 1.39 us
    pallas_call x1, Pallas kernels: 76 us -> 66.1 us  [on_device(): pl.pallas_call(functools.partial(kernel, grid), out_shape=jax.ShapeDtypeS...]
    unnamed x2 -> x1, local copies, waits for them, and re-layouts: 2.8 us -> 1.39 us
where the time goes in v4:
time: 67.7 us; the launch traced here: 67.5 us
  Pallas kernels  66.1 us (98%)
  local copies, waits for them, and re-layouts  1.39 us (2%)
    pallas_call x1, Pallas kernels, on_device(): pl.pallas_call(functools.partial(kernel, grid), out_shape=jax.ShapeDtypeS...  66.1 us
    unnamed x1, local copies, waits for them, and re-layouts  1.39 us

profile of v4, /device:TPU:1, one launch (start us, length us, event | category | flops | bytes accessed | tf_op | source)
XLA Modules:
  0.0 67.5 jit_solution(6752173841208795939)
XLA Ops:
  0.0 66.1 %multipole.1 = bf16[32,1,4,128]{3,2,1,0:T(4,128)(2,1)} custom-call(bf16[32,192]{1,0:T(8,128)(2,1)} %bitcast.4, bf16[32,4,128]{2,1,0:T(4,128)(2,1)} %bitcast.3, s32[32,27]{1,0:T(8,128)} %near_box_ref.1, s32[32,27]{1,0:T(8,128)} %near_code_ref.1, s32[16,128]{1,0:T(8,128)} %bitcast.5, s32[32,128]{1,0:T(8,128)} %slot_hbm.1, s32[32,128]{1,0:T(8,128)} %slot_dir_hbm.1, ...), custom_call_target="tpu_custom_call" | custom-call | flops 5000000000 | bytes 10000000 | tf_op jit(solution)/shard_map/multipole/pallas_call | solution.py:727
  66.1 1.4 %copy.17 = bf16[32,1,4,128]{3,2,1,0:T(4,128)(2,1)} copy(bf16[32,1,4,128]{3,2,1,0:T(4,128)(2,1)} %multipole.1) | data formatting | bytes 65536

commit v5 on v4

--- a/solution.py
+++ b/solution.py
@@ -315,7 +315,7 @@
         hot_ref[rows_at(t * 16, 16), :] = slots_of(t, first_slots)
         return carry
 
-    lax.fori_loop(0, peers, mark, 0, unroll=8)
+    lax.fori_loop(0, peers, mark, 0, unroll=min(16, peers))
     for index in range(5):
         hot_near_ref[pl.ds(index * 16, 16), :] = slots_of(around(index - REACH), last_slots)
     recv_buf[pl.ds((peers + 5) * 16, 48), :] = jnp.zeros((48, 256), BF16)
@@ -366,7 +366,7 @@
         raised_ref[rows_at(b * 8, 8), :] = dot(charges_at(HB + b), tile)[:8]
         return carry
 
-    lax.fori_loop(0, BOX_DEV, raise_box, 0, unroll=8)
+    lax.fori_loop(0, BOX_DEV, raise_box, 0, unroll=16)
     outgoing = []
     for r in range(2):
         pieces = [
@@ -382,7 +382,7 @@
         send_buf[rows, :] = dot(hot_ref[rows, :], outgoing).astype(BF16)
         return carry
 
-    lax.fori_loop(0, blocks, fill, 0, unroll=min(4, blocks))
+    lax.fori_loop(0, blocks, fill, 0, unroll=blocks)
     send_near[...] = dot(hot_near_ref[...], outgoing).astype(BF16)
 
     def leaf_copy(t):
@@ -575,7 +575,7 @@
         far_ref[rows_at(pair * 256, 256), :] = jnp.concatenate([real, imag], axis=0)
         return carry
 
-    lax.fori_loop(0, HALF_BOX, lower, 0, unroll=8)
+    lax.fori_loop(0, HALF_BOX, lower, 0, unroll=16)
 
     for copy in list_copies[1:]:
         copy.wait()
@@ -599,7 +599,7 @@
                 ]
         return carry
 
-    lax.fori_loop(0, BOX_DEV, count_slots, 0, unroll=4)
+    lax.fori_loop(0, BOX_DEV, count_slots, 0, unroll=8)
 
     coarse_head = iota((blocks * 16, 32), 0)
     coarse_tail = iota((512, 32), 0)
@@ -692,7 +692,7 @@
         out_ref[2 * pair + 1, 0] = jnp.where(low_lane, turned[8:12], total[12:16]).astype(BF16)
         return carry
 
-    lax.fori_loop(0, HALF_BOX, finish, 0, unroll=8)
+    lax.fori_loop(0, HALF_BOX, finish, 0, unroll=16)
 
     for copy in pair_copies + halo_copies + close_copies + [near_copy, local_copy]:
         copy.wait_send()

time: 67.7 us -> 67 us (0.990)
  Pallas kernels: 66.1 us -> 65.3 us
    pallas_call x1, Pallas kernels: 66.1 us -> 65.3 us  [on_device(): pl.pallas_call(functools.partial(kernel, grid), out_shape=jax.ShapeDtypeS...]
where the time goes in v5:
time: 67 us; the launch traced here: 66.7 us
  Pallas kernels  65.3 us (97%)
  local copies, waits for them, and re-layouts  1.39 us (2%)
    pallas_call x1, Pallas kernels, on_device(): pl.pallas_call(functools.partial(kernel, grid), out_shape=jax.ShapeDtypeS...  65.3 us
    unnamed x1, local copies, waits for them, and re-layouts  1.39 us

profile of v5, /device:TPU:1, one launch (start us, length us, event | category | flops | bytes accessed | tf_op | source)
XLA Modules:
  0.0 66.7 jit_solution(12937631625892804819)
XLA Ops:
  0.0 65.3 %multipole.1 = bf16[32,1,4,128]{3,2,1,0:T(4,128)(2,1)} custom-call(bf16[32,192]{1,0:T(8,128)(2,1)} %bitcast.4, bf16[32,4,128]{2,1,0:T(4,128)(2,1)} %bitcast.3, s32[32,27]{1,0:T(8,128)} %near_box_ref.1, s32[32,27]{1,0:T(8,128)} %near_code_ref.1, s32[16,128]{1,0:T(8,128)} %bitcast.5, s32[32,128]{1,0:T(8,128)} %slot_hbm.1, s32[32,128]{1,0:T(8,128)} %slot_dir_hbm.1, ...), custom_call_target="tpu_custom_call" | custom-call | flops 5000000000 | bytes 10000000 | tf_op jit(solution)/shard_map/multipole/pallas_call | solution.py:727
  65.3 1.4 %copy.17 = bf16[32,1,4,128]{3,2,1,0:T(4,128)(2,1)} copy(bf16[32,1,4,128]{3,2,1,0:T(4,128)(2,1)} %multipole.1) | data formatting | bytes 65536
